TPU v7x, 32 devices: a whole 2x2x4 slice. The times are simulated.
32 devices in a mesh: row: 4 (over y, x), col: 8 (over z, core).
Axes of the slice: x: 2, y: 2, z: 4, core: 2. Of those that a mesh axis runs over, the one named last changes fastest.
Arguments:
- rhs: float32 [4, 4, 512, 2, 8, 512], P(None, 'row', None, None, 'col'), may hold values from -6 to 6, as said below
- panels: bfloat16 [2, 4, 4, 512, 1024], P(None, None, 'row', 'col'), may hold values from -6 to 6, as said below
- inverses: float32 [3, 512, 512], replicated, may hold values from -2 to 2, as said below
Outputs:
- new_rhs: float32 [4, 4, 512, 2, 8, 512], P(None, 'row', None, None, 'col')
- solved: float32 [2, 512, 512], P(None, 'row', 'col')
Inputs may be any that keep to these rules, and one draw needn't show every extreme that they name: rhs is symmetric as a matrix of order 16 * 512. `panels`: A and E are upper triangular: panel rows of block n are zero in the first 512 columns, and the diagonal blocks (m,m) and (n,n) are upper triangular with positive diagonals. The inverses are upper triangular preconditioners, only near the true inverses, and are used as given.
All inputs are finite; a program needn't handle non-finite values.
Results may differ from a plain program's by a relative error of at most 0.0025.
Values may be sent and summed in bfloat16 or wider, within the bound.
A program may use at most 128 MiB of HBM per device.

v0:
```python
import jax
import jax.numpy as jnp
from jax import lax
from jax.sharding import PartitionSpec as P

SWEEPS = 3


def spread(value, axis, source):
    kept = jnp.where(lax.axis_index(axis) == source, value, 0).astype(value.dtype)
    return lax.psum(kept, axis)


def product(left, right):
    return jnp.dot(left, right, precision=lax.Precision.HIGHEST, preferred_element_type=jnp.float32)


def solve_corner(corner, rhs_block, inverses):
    half_cols = corner.shape[-1] // 2
    a_last = corner[0, :, half_cols:].astype(jnp.float32)
    e_last = corner[1, :, half_cols:].astype(jnp.float32)
    solution = jnp.zeros(rhs_block.shape, jnp.float32)
    for sweep_index in range(SWEEPS):
        left_term = product(product(a_last, solution), e_last.T)
        residual = -rhs_block - (left_term + left_term.T)
        update_term = product(product(inverses[1], residual), inverses[2].T)
        solution = solution + 0.25 * (update_term + update_term.T)
    return solution


def skip_corner(corner, rhs_block, inverses):
    return jnp.zeros(rhs_block.shape, jnp.float32)


def solve_upper(corner, lower_diag, diag_solution, rhs_block, inverses):
    half_cols = corner.shape[-1] // 2
    a_diag = corner[0, :, :half_cols].astype(jnp.float32)
    e_diag = corner[1, :, :half_cols].astype(jnp.float32)
    a_upper = corner[0, :, half_cols:].astype(jnp.float32)
    e_upper = corner[1, :, half_cols:].astype(jnp.float32)
    a_last = lower_diag[0]
    e_last = lower_diag[1]
    target = -rhs_block - (
        product(product(a_upper, diag_solution), e_last.T)
        + product(product(e_upper, diag_solution), a_last.T)
    )
    solution = jnp.zeros(rhs_block.shape, jnp.float32)
    for sweep_index in range(SWEEPS):
        residual = target - (
            product(product(a_diag, solution), e_last.T)
            + product(product(e_diag, solution), a_last.T)
        )
        solution = solution + 0.5 * product(product(inverses[0], residual), inverses[2].T)
    return solution


def skip_upper(corner, lower_diag, diag_solution, rhs_block, inverses):
    return jnp.zeros(rhs_block.shape, jnp.float32)


def pick_columns(gathered, col_index, row_count, col_count, count):
    chosen = [
        lax.dynamic_index_in_dim(
            gathered, col_index // row_count + column_block * (col_count // row_count), 1, False
        )
        for column_block in range(count)
    ]
    return jnp.stack(chosen, 1)


def send_columns(chosen, col_index, row_count):
    return spread(chosen, "row", col_index % row_count)


def on_device(rhs, panels, inverses):
    row_index = lax.axis_index("row")
    col_index = lax.axis_index("col")
    row_count = lax.axis_size("row")
    col_count = lax.axis_size("col")
    blocks_here = panels.shape[1]
    col_blocks = rhs.shape[3]
    block_size = rhs.shape[-1]
    local_panels = panels[:, :, 0]
    gathered = lax.all_gather(local_panels, "col", axis=2, tiled=True)
    corner = gathered[:, blocks_here - 1]
    received = send_columns(
        pick_columns(gathered, col_index, row_count, col_count, col_blocks), col_index, row_count
    )
    rhs_last = rhs[blocks_here - 1, 0, :, col_blocks - 1, 0, :]
    last_col = col_index == col_count - 1
    diag_solution = lax.cond(
        jnp.logical_and(last_col, row_index == row_count - 1),
        solve_corner,
        skip_corner,
        corner,
        rhs_last,
        inverses,
    )
    corner_pack = jnp.stack(
        [
            diag_solution,
            corner[0, :, block_size:].astype(jnp.float32),
            corner[1, :, block_size:].astype(jnp.float32),
        ]
    )
    corner_pack = spread(corner_pack, ("row", "col"), (row_count - 1) * col_count + col_count - 1)
    diag_here = corner_pack[0]
    lower_diag = corner_pack[1:3]
    next_solution = lax.cond(
        jnp.logical_and(last_col, row_index == row_count - 2),
        solve_upper,
        skip_upper,
        corner,
        lower_diag,
        diag_here,
        rhs_last,
        inverses,
    )
    next_solution = spread(
        next_solution, ("row", "col"), (row_count - 2) * col_count + col_count - 1
    )
    solution_blocks = jnp.stack([diag_here, next_solution])
    rows_part = block_size // row_count
    cols_part = block_size // col_count
    solved = lax.dynamic_slice(
        solution_blocks,
        (0, row_index * rows_part, col_index * cols_part),
        (2, rows_part, cols_part),
    )
    zero_block = jnp.zeros((block_size, block_size), jnp.float32)
    upper_half = jnp.concatenate([zero_block, next_solution], 1)
    lower_half = jnp.concatenate([next_solution.T, diag_here], 1)
    known_block = jnp.concatenate([upper_half, lower_half], 0).astype(jnp.bfloat16)
    unknown_rows = jnp.einsum(
        "akm,mn->akn", gathered[0], known_block, preferred_element_type=jnp.float32
    ).astype(jnp.bfloat16)
    second_matrix_rows = gathered[1]
    unknown_columns = jnp.einsum(
        "akm,mn->akn", received[0], known_block, preferred_element_type=jnp.float32
    ).astype(jnp.bfloat16)
    second_matrix_columns = received[1]
    update_block = jnp.einsum(
        "wzt,ljt->wzlj", unknown_rows, second_matrix_columns, preferred_element_type=jnp.float32
    )
    update_block = update_block + jnp.einsum(
        "wzt,ljt->wzlj", second_matrix_rows, unknown_columns, preferred_element_type=jnp.float32
    )
    new_rhs = rhs + update_block[:, None, :, :, None, :]
    return (new_rhs, solved)


def solution(mesh):
    in_specs = (P(None, "row", None, None, "col", None), P(None, None, "row", "col", None), P())
    out_specs = (P(None, "row", None, None, "col", None), P(None, "row", "col"))
    return jax.shard_map(
        on_device, mesh=mesh, in_specs=in_specs, out_specs=out_specs, check_vma=False
    )
```

profile of v0, /device:TPU:18, one launch (start us, length us, event | category | flops | bytes accessed | tf_op | source)
XLA Modules:
  0.0 654.2 jit_solution(17926451010706732757)
XLA Ops:
  7.2 0.0 all-gather.3.cloned.1.call-start
  7.2 0.7 all-gather.3.cloned.1.call-update
  7.9 0.0 all-reduce.5.cloned.1.call-start
  8.0 1.9 slice.75
  9.9 0.1 copy.39
  10.0 81.3 %all-gather.3.cloned.1.call-done = bf16[2,4,1,512,1024]{4,3,1,2,0:T(8,128)(2,1)} async-done(((bf16[2,4,1,64,1024]{4,3,1,2,0:T(8,128)(2,1)}), bf16[2,4,1,512,1024]{4,3,1,2,0:T(8,128)(2,1)}) %all-gather.3.cloned.1.call-update) | async-done | bytes 8388624 | tf_op jit(solution)/shard_map/all_gather | solution.py:84
  91.3 1.8 slice_bitcast_fusion.12
  93.0 1.6 slice_convert_fusion.1
  94.6 10.4 %conditional.2 = (f32[1,512,512]{2,1,0:T(8,128)}) conditional(s32[]{:T(128)} %convert_element_type.37, () %tuple.23, (f32[512,512]{1,0:T(8,128)S(1)}, bf16[2,512,1024]{2,1,0:T(8,128)(2,1)S(1)}, f32[3,512,512]{2,1,0:T(8,128)}) %tuple.45), branch_computations={%region_0.1_spmd, %region_1.2_spmd} | conditional | flops 19332333568 | bytes 67108904 | solution.py:91
  94.6 1.2 stack.7
  105.1 4.0 maximum_select_fusion.1
  109.1 0.0 all-reduce.5.cloned.1.call-update
  109.1 0.0 all-reduce.7.cloned.1.call-start
  109.2 197.2 %all-reduce.5.cloned.1.call-done = f32[3,512,512]{2,1,0:T(8,128)} async-done(((f32[3,512,512]{2,1,0:T(8,128)}), f32[3,512,512]{2,1,0:T(8,128)}) %all-reduce.5.cloned.1.call-update) | async-done | bytes 3145744 | tf_op jit(solution)/shard_map/psum | solution.py:11
  306.3 3.0 fusion.153
  309.3 7.5 %conditional.3 = (f32[512,512]{1,0:T(8,128)S(1)}) conditional(s32[]{:T(128)} %convert_element_type.36, () %tuple.22, (f32[512,512]{1,0:T(8,128)S(1)}, bf16[2,512,1024]{2,1,0:T(8,128)(2,1)S(1)}, f32[512,512]{1,0:T(8,128)}, f32[3,512,512]{2,1,0:T(8,128)}, f32[3,512,512]{2,1,0:T(8,128)}) %tuple.46), branch_computations={%region_3.4_spmd, %region_4.5_spmd} | conditional | flops 35437150208 | bytes 98566208 | solution.py:109
  309.3 0.1 broadcast.18
  316.9 1.1 broadcast_select_fusion
  317.9 0.0 all-reduce.7.cloned.1.call-update
  317.9 0.0 all-reduce.9.cloned.1.call-start
  318.0 2.7 dynamic-slice_bitcast_fusion.1
  320.7 2.3 maximum_select_fusion
  323.0 0.0 copy-start.2
  323.0 0.0 copy-start.5
  323.0 0.0 all-reduce.9.cloned.1.call-update
  323.0 1.2 copy-done.2
  324.2 0.2 copy.28
  324.4 174.2 %all-reduce.7.cloned.1.call-done = f32[512,512]{1,0:T(8,128)} async-done(((f32[512,512]{1,0:T(8,128)}), f32[512,512]{1,0:T(8,128)}) %all-reduce.7.cloned.1.call-update) | async-done | bytes 1048592 | tf_op jit(solution)/shard_map/psum | solution.py:11
  498.6 0.0 copy-start.3
  498.6 0.0 copy-done.5
  498.6 1.0 fusion.143
  499.7 0.7 copy.32
  500.4 0.0 copy-done.3
  500.4 0.1 convert.11
  500.5 0.2 copy.27
  500.7 0.1 convert_bitcast_fusion
  500.7 105.5 %all-reduce.9.cloned.1.call-done = bf16[2,2,512,1024]{3,2,1,0:T(8,128)(2,1)} async-done(((bf16[2,2,512,1024]{3,2,1,0:T(8,128)(2,1)}), bf16[2,2,512,1024]{3,2,1,0:T(8,128)(2,1)}) %all-reduce.9.cloned.1.call-update) | async-done | bytes 4194320 | tf_op jit(solution)/shard_map/psum | solution.py:11
  606.2 3.9 fusion.134
  610.1 9.0 %fusion.124 = f32[2,512,4,512]{1,3,0,2:T(8,128)} fusion(bf16[2,4,1,512,1024]{4,3,1,2,0:T(8,128)(2,1)} %all-gather.3.cloned.1.call-done, bf16[2,512,1024]{2,1,0:T(8,128)(2,1)S(1)} %fusion.134), kind=kOutput, calls=%fused_computation.136 | convolution fusion | flops 4294967296 | bytes 14680064 | tf_op jit(solution)/shard_map/wzt,ljt->wzlj/dot_general | solution.py:145
  619.1 17.4 %bitcast_add_fusion.6 = f32[4,1,512,2,1,512]{5,2,3,0,4,1:T(8,128)} fusion(f32[2,512,4,512]{1,3,0,2:T(8,128)} %fusion.124, f32[4,1,512,2,1,512]{5,4,3,2,1,0:T(1,128)} %param.7, bf16[2,2,512,1024]{3,2,1,0:T(8,128)(2,1)} %all-reduce.9.cloned.1.call-done, bf16[2,4,1,512,1024]{4,3,1,2,0:T(8,128)(2,1)} %all-gather.3.cloned.1.call-done, ...), kind=kOutput, calls=%fused_computation.133 | convolution fusion | flops 8604614656 | bytes 33030144 | tf_op jit(solution)/shard_map/wzt,ljt->wzlj/dot_general | solution.py:142
  636.5 11.0 %copy.31 = f32[4,1,512,2,1,512]{5,4,3,2,1,0:T(1,128)} copy(f32[4,1,512,2,1,512]{5,2,3,0,4,1:T(8,128)} %bitcast_add_fusion.6) | data formatting | bytes 16777216
Async XLA Ops:
  7.2 84.1 %all-gather.3.cloned.1.call-start = ((), (), s32[]{:S(2)}) async-start(), calls=%async_computation.3 | async-start | bytes 9437184 | tf_op jit(solution)/shard_map/all_gather | solution.py:84
  7.9 298.4 %all-reduce.5.cloned.1.call-start = ((), (), s32[]{:S(2)}) async-start(), calls=%async_computation | async-start | bytes 6291456 | tf_op jit(solution)/shard_map/psum | solution.py:11
  109.1 389.5 %all-reduce.7.cloned.1.call-start = ((), (), s32[]{:S(2)}) async-start(), calls=%async_computation.1 | async-start | bytes 2097152 | tf_op jit(solution)/shard_map/psum | solution.py:11
  317.9 288.3 %all-reduce.9.cloned.1.call-start = ((), (), s32[]{:S(2)}) async-start(), calls=%async_computation.2 | async-start | bytes 8388608 | tf_op jit(solution)/shard_map/psum | solution.py:11
  323.0 1.2 copy-start.2
  323.0 175.6 %copy-start.5 = (f32[1,512,512]{2,1,0:T(8,128)S(1)}, f32[1,512,512]{2,1,0:T(8,128)}, u32[]{:S(2)}) copy-start(f32[1,512,512]{2,1,0:T(8,128)} %get-tuple-element.45) | copy-start | bytes 3145732
  498.6 1.8 copy-start.3
Sparse Core Ops, SparseCore 0:
  9.6 81.6 all-gather.2
  109.2 197.0 all-reduce.4
  318.1 180.5 all-reduce.6
  502.3 103.8 all-reduce.8
where the time goes:
time: 666 us; the launch traced here: 654 us
  waiting for transfers between devices  559 us (84%)
  matrix products  30.3 us (5%)
  local copies, waits for them, and re-layouts  24.1 us (4%)
  loops' own time  16.7 us (3%)
  between operations  14.1 us (2%)
  other arithmetic  10.1 us (2%)
    psum x3, waiting for transfers between devices, spread(): return lax.psum(kept, axis)  477 us
    all_gather x1, waiting for transfers between devices, on_device(): gathered = lax.all_gather(local_panels, 'col', axis=2, tiled=True)  81.3 us
    dot_general x1, matrix products, on_device(): jnp.einsum('wzt,ljt->wzlj', unknown_rows, second_matrix_columns, preferre...  17.4 us
  transfers between devices with their start and end apart: 4, of which 4 were waited for; matrix products, arithmetic and copies ran while one was open for 1% of the time, Pallas kernels for 0%

commit v1 on v0

v1 whole, which is shorter than its diff:
```python
import functools

import jax
import jax.numpy as jnp
from jax import lax
from jax.experimental import pallas as pl
from jax.experimental.pallas import tpu as pltpu
from jax.sharding import PartitionSpec as P

SWEEPS = 3
LANES = 128
MESH = pl.DeviceIdType.MESH
VMEM_LIMIT = 50 * 1024 * 1024


def remote(src, dst, send_sem, recv_sem, row, col):
    return pltpu.make_async_remote_copy(
        src_ref=src, dst_ref=dst, send_sem=send_sem, recv_sem=recv_sem,
        device_id=(row, col), device_id_type=MESH,
    )


def greet(partners):
    barrier = pltpu.get_barrier_semaphore()
    for row, col in partners:
        pl.semaphore_signal(barrier, inc=1, device_id=(row, col), device_id_type=MESH)
    pl.semaphore_wait(barrier, len(partners))


def corner_kernel(
    row_count, col_count, last_ref, g_ref, upper, lower, g_out,
    send_upper, send_lower, send_sibling, send_g1, send_g2, send_g3, send_g4,
    recv_corner, recv_sibling, recv_g1, recv_g2, recv_g3, recv_g4, local_sem,
):
    row = lax.axis_index("row")
    col = lax.axis_index("col")
    core = lax.rem(col, 2)
    sibling = col + 1 - 2 * core
    size = g_ref.shape[0]
    half = size // 2
    part = size // row_count
    last_col = col_count - 1
    other_rows = [lax.rem(row + j, row_count) for j in range(1, row_count)]
    other_cols = [lax.rem(col + 2 * j, col_count) for j in range(1, col_count // 2)]
    greet([(r, col) for r in other_rows] + [(row, c) for c in other_cols] + [(row, sibling)])

    here = pl.ds(pl.multiple_of(core * half, half), half)
    there = pl.ds(pl.multiple_of((1 - core) * half, half), half)

    def rows_of(index):
        return pl.ds(pl.multiple_of(index * part, part), part)

    corners = (
        (row_count - 2, last_ref.at[:, here, :], upper, send_upper, 0),
        (row_count - 1, last_ref.at[:, here, pl.ds(size, size)], lower, send_lower, 1),
    )
    for source_row, src, out, send, slot in corners:
        dst = out.at[:, here, :]

        @pl.when(row == source_row)
        def _():
            pltpu.make_async_copy(src, dst, local_sem.at[slot]).start()
            for j, r in enumerate(other_rows):
                remote(src, dst, send.at[j], recv_corner.at[slot], r, col).start()

        @pl.when(jnp.logical_and(row == source_row, col == last_col))
        def _():
            mine = rows_of(row)
            pltpu.make_async_copy(
                g_ref.at[mine, :], g_out.at[slot, mine, :], local_sem.at[2 + slot]
            ).start()
            for j, r in enumerate(other_rows):
                theirs = rows_of(r)
                remote(
                    g_ref.at[theirs, :], g_out.at[slot, theirs, :],
                    send_g1.at[slot, j], recv_g1.at[slot], r, col,
                ).start()

    mine = rows_of(row)
    g_mine = g_out.at[:, mine, :]

    @pl.when(col == last_col)
    def _():
        for source_row, src, out, send, slot in corners:
            piece = g_out.at[slot, mine, :]

            @pl.when(row == source_row)
            def _():
                pltpu.make_async_copy(g_ref.at[mine, :], piece, local_sem.at[2 + slot]).wait()

            @pl.when(row != source_row)
            def _():
                remote(piece, piece, send_g1.at[slot, 0], recv_g1.at[slot], row, col).wait_recv()

        for j, c in enumerate(other_cols):
            remote(g_mine, g_mine, send_g2.at[j], recv_g2, row, c).start()

    for source_row, src, out, send, slot in corners:
        dst = out.at[:, here, :]

        @pl.when(row == source_row)
        def _():
            pltpu.make_async_copy(src, dst, local_sem.at[slot]).wait()

        @pl.when(row != source_row)
        def _():
            remote(dst, dst, send.at[0], recv_corner.at[slot], row, col).wait_recv()

        remote(dst, dst, send_sibling.at[slot], recv_sibling.at[slot], row, sibling).start()

    @pl.when(core == 1)
    def _():
        @pl.when(col != last_col)
        def _():
            remote(g_mine, g_mine, send_g2.at[0], recv_g2, row, col).wait_recv()

        for j, r in enumerate(other_rows):
            remote(g_mine, g_mine, send_g3.at[j], recv_g3.at[row], r, col).start()
        for r in other_rows:
            piece = g_out.at[:, rows_of(r), :]
            remote(piece, piece, send_g3.at[0], recv_g3.at[r], row, col).wait_recv()
        remote(g_out, g_out, send_g4, recv_g4, row, sibling).start()

    @pl.when(core == 0)
    def _():
        remote(g_out, g_out, send_g4, recv_g4, row, sibling).wait_recv()

    for source_row, src, out, send, slot in corners:
        dst = out.at[:, here, :]
        arriving = out.at[:, there, :]
        remote(arriving, arriving, send_sibling.at[slot], recv_sibling.at[slot], row, sibling).wait_recv()
        remote(dst, dst, send_sibling.at[slot], recv_sibling.at[slot], row, sibling).wait_send()

        @pl.when(row == source_row)
        def _():
            for j, r in enumerate(other_rows):
                remote(src, dst, send.at[j], recv_corner.at[slot], r, col).wait_send()

        @pl.when(jnp.logical_and(row == source_row, col == last_col))
        def _():
            for j, r in enumerate(other_rows):
                theirs = rows_of(r)
                remote(
                    g_ref.at[theirs, :], g_out.at[slot, theirs, :],
                    send_g1.at[slot, j], recv_g1.at[slot], r, col,
                ).wait_send()

    @pl.when(col == last_col)
    def _():
        for j, c in enumerate(other_cols):
            remote(g_mine, g_mine, send_g2.at[j], recv_g2, row, c).wait_send()

    @pl.when(core == 1)
    def _():
        for j, r in enumerate(other_rows):
            remote(g_mine, g_mine, send_g3.at[j], recv_g3.at[row], r, col).wait_send()
        remote(g_out, g_out, send_g4, recv_g4, row, sibling).wait_send()


def share_corner(last_rows, rhs_last, row_count, col_count):
    size = rhs_last.shape[0]
    dma = pltpu.SemaphoreType.DMA
    peers = row_count - 1
    return pl.pallas_call(
        functools.partial(corner_kernel, row_count, col_count),
        out_shape=(
            jax.ShapeDtypeStruct((2, size, 2 * size), jnp.bfloat16),
            jax.ShapeDtypeStruct((2, size, size), jnp.bfloat16),
            jax.ShapeDtypeStruct((2, size, size), jnp.float32),
        ),
        in_specs=[pl.BlockSpec(memory_space=pl.ANY)] * 2,
        out_specs=[pl.BlockSpec(memory_space=pl.ANY)] * 3,
        scratch_shapes=[
            dma((peers,)), dma((peers,)), dma((2,)), dma((2, peers)),
            dma((col_count // 2,)), dma((peers,)), dma,
            dma((2,)), dma((2,)), dma((2,)), dma, dma((row_count,)), dma, dma((4,)),
        ],
        compiler_params=pltpu.CompilerParams(collective_id=0, has_side_effects=True),
        cost_estimate=pl.CostEstimate(flops=0, bytes_accessed=60_000_000, transcendentals=0),
    )(last_rows, rhs_last)


def mm(left, right):
    return lax.dot_general(left, right, (((1,), (0,)), ((), ())), preferred_element_type=jnp.float32)


def mm_t(left, right):
    return lax.dot_general(left, right, (((1,), (1,)), ((), ())), preferred_element_type=jnp.float32)


def split(value):
    high = value.astype(jnp.bfloat16)
    low = (value - high.astype(jnp.float32)).astype(jnp.bfloat16)
    return high, low


def upper_times(tri, parts):
    half = tri[0].shape[0] // 2
    top = bottom = None
    for i, t in enumerate(tri):
        for j, p in enumerate(parts):
            if i + j < 2:
                a = mm(t[:half], p)
                b = mm(t[half:, half:], p[half:])
                top = a if top is None else top + a
                bottom = b if bottom is None else bottom + b
    return jnp.concatenate([top, bottom], 0)


def times_upper_t(parts, tri):
    half = tri[0].shape[0] // 2
    left = right = None
    for i, t in enumerate(tri):
        for j, p in enumerate(parts):
            if i + j < 2:
                a = mm_t(p, t[:half])
                b = mm_t(p[:, half:], t[half:, half:])
                left = a if left is None else left + a
                right = b if right is None else right + b
    return jnp.concatenate([left, right], 1)


def solve_kernel(upper, lower, g, inverses, out, inv_high, inv_low):
    size = g.shape[1]
    for i in range(3):
        high, low = split(inverses[i])
        inv_high[i] = high
        inv_low[i] = low

    def precondition(i, residual):
        first = upper_times((inv_high[i], inv_low[i]), split(residual))
        return times_upper_t(split(first), (inv_high[2], inv_low[2]))

    def corner_update(residual):
        update = precondition(1, residual)
        return 0.25 * (update + update.T)

    out[0] = corner_update(-g[1])

    def corner_sweep(_, carry):
        first = upper_times((lower[0],), split(out[0]))
        term = times_upper_t(split(first), (lower[1],))
        out[0] = out[0] + corner_update(-g[1] - (term + term.T))
        return carry

    lax.fori_loop(1, SWEEPS, corner_sweep, 0)

    parts = split(out[0])
    over_a = split(sum(mm(upper[0, :, size:], p) for p in parts))
    over_e = split(sum(mm(upper[1, :, size:], p) for p in parts))
    g[0] = -g[0] - (times_upper_t(over_a, (lower[1],)) + times_upper_t(over_e, (lower[0],)))
    out[1] = 0.5 * precondition(0, g[0])

    def upper_sweep(_, carry):
        held = split(out[1])
        by_a = split(upper_times((upper[0, :, :size],), held))
        by_e = split(upper_times((upper[1, :, :size],), held))
        term = times_upper_t(by_a, (lower[1],)) + times_upper_t(by_e, (lower[0],))
        out[1] = out[1] + 0.5 * precondition(0, g[0] - term)
        return carry

    lax.fori_loop(1, SWEEPS, upper_sweep, 0)


def solve(upper, lower, g, inverses):
    size = g.shape[1]
    return pl.pallas_call(
        solve_kernel,
        out_shape=jax.ShapeDtypeStruct((2, size, size), jnp.float32),
        in_specs=[pl.BlockSpec(memory_space=pltpu.VMEM)] * 4,
        out_specs=pl.BlockSpec(memory_space=pltpu.VMEM),
        scratch_shapes=[
            pltpu.VMEM((3, size, size), jnp.bfloat16),
            pltpu.VMEM((3, size, size), jnp.bfloat16),
        ],
        compiler_params=pltpu.CompilerParams(vmem_limit_bytes=VMEM_LIMIT),
        cost_estimate=pl.CostEstimate(
            flops=100 * size ** 3, bytes_accessed=100_000_000, transcendentals=0
        ),
    )(upper, lower, g, inverses)


def gray(index):
    return index ^ (index >> 1)


def column_kernel(row_count, chosen, out, send, recv, local_sem):
    row = lax.axis_index("row")
    col = lax.axis_index("col")
    source = lax.rem(col, row_count)
    matrices, blocks, size, _ = chosen.shape
    part = size // 4
    chunks = [
        (m, b, pl.ds(p * part, part)) for b in range(blocks) for p in range(4) for m in range(matrices)
    ]
    places = [gray(i) for i in range(row_count)]

    def at_place(place):
        value = jnp.int32(0)
        for s in range(row_count):
            value = jnp.where(source == s, s ^ places[place], value)
        return value

    chain = [at_place(i) for i in range(row_count)]
    barrier = pltpu.get_barrier_semaphore()
    for i in range(row_count):

        @pl.when(row == chain[i])
        def _():
            around = [chain[j] for j in (i - 1, i + 1) if 0 <= j < row_count]
            for r in around:
                pl.semaphore_signal(barrier, inc=1, device_id=(r, col), device_id_type=MESH)
            pl.semaphore_wait(barrier, len(around))
            if i == 0:
                pltpu.make_async_copy(chosen, out, local_sem).start()
            for n, (m, b, rows) in enumerate(chunks):
                dst = out.at[m, b, rows, :]
                src = chosen.at[m, b, rows, :] if i == 0 else dst
                if i > 0:
                    remote(dst, dst, send.at[n], recv.at[n], row, col).wait_recv()
                if i < row_count - 1:
                    remote(src, dst, send.at[n], recv.at[n], chain[i + 1], col).start()
            if i == 0:
                pltpu.make_async_copy(chosen, out, local_sem).wait()
            if i < row_count - 1:
                for n, (m, b, rows) in enumerate(chunks):
                    dst = out.at[m, b, rows, :]
                    src = chosen.at[m, b, rows, :] if i == 0 else dst
                    remote(src, dst, send.at[n], recv.at[n], chain[i + 1], col).wait_send()


def share_columns(chosen, row_count):
    count = chosen.shape[0] * chosen.shape[1] * 4
    dma = pltpu.SemaphoreType.DMA
    return pl.pallas_call(
        functools.partial(column_kernel, row_count),
        out_shape=jax.ShapeDtypeStruct(chosen.shape, chosen.dtype),
        in_specs=[pl.BlockSpec(memory_space=pl.ANY)],
        out_specs=pl.BlockSpec(memory_space=pl.ANY),
        scratch_shapes=[dma((count,)), dma((count,)), dma],
        compiler_params=pltpu.CompilerParams(collective_id=1, has_side_effects=True),
        cost_estimate=pl.CostEstimate(flops=0, bytes_accessed=60_000_000, transcendentals=0),
    )(chosen)


def update_kernel(
    rest_steps, rest_ref, last_ref, cols_ref, x_ref, rhs_ref, out_ref, x_high, x_turned, z_cols
):
    step = pl.program_id(0)
    size = x_ref.shape[1]
    tile = rest_ref.shape[1]
    groups = rhs_ref.shape[0] // tile

    def times_known(left):
        from_right = left[:, size:]
        first = mm(from_right, x_turned[...])
        second = mm(left[:, :size], x_high[1]) + mm(from_right, x_high[0])
        return jnp.concatenate([first, second], 1).astype(jnp.bfloat16)

    @pl.when(step == 0)
    def _():
        x_high[...] = x_ref[...].astype(jnp.bfloat16)
        x_turned[...] = x_ref[1].T.astype(jnp.bfloat16)
        for b in range(z_cols.shape[0]):
            z_cols[b] = times_known(cols_ref[0, b])

    def work(rows_ref):
        z_rows = times_known(rows_ref[0])
        for b in range(z_cols.shape[0]):
            total = mm_t(z_rows, cols_ref[1, b]) + mm_t(rows_ref[1], z_cols[b])
            for q in range(size // LANES):
                where = pl.ds(b * (size // LANES) + q, tile, stride=groups)
                out_ref[where, :] = rhs_ref[where, :] + total[:, q * LANES:(q + 1) * LANES]

    @pl.when(step < rest_steps)
    def _():
        work(rest_ref)

    @pl.when(step >= rest_steps)
    def _():
        work(last_ref)


def update(rest, last, cols, x, rhs):
    size = x.shape[1]
    width = rest.shape[-1]
    blocks = cols.shape[1]
    rest_rows = rest.reshape(2, -1, width)
    tile = size // 2
    groups = blocks * size // LANES
    rest_steps = rest_rows.shape[1] // tile
    steps = rest_steps + last.shape[1] // tile
    flat = rhs.reshape(-1, LANES)
    out = pl.pallas_call(
        functools.partial(update_kernel, rest_steps),
        grid=(steps,),
        out_shape=jax.ShapeDtypeStruct(flat.shape, flat.dtype),
        in_specs=[
            pl.BlockSpec((2, tile, width), lambda i: (0, jnp.minimum(i, rest_steps - 1), 0)),
            pl.BlockSpec((2, tile, width), lambda i: (0, jnp.maximum(i - rest_steps, 0), 0)),
            pl.BlockSpec(cols.shape, lambda i: (0, 0, 0, 0)),
            pl.BlockSpec(x.shape, lambda i: (0, 0, 0)),
            pl.BlockSpec((tile * groups, LANES), lambda i: (i, 0)),
        ],
        out_specs=pl.BlockSpec((tile * groups, LANES), lambda i: (i, 0)),
        scratch_shapes=[
            pltpu.VMEM((2, size, size), jnp.bfloat16),
            pltpu.VMEM((size, size), jnp.bfloat16),
            pltpu.VMEM((blocks, size, width), jnp.bfloat16),
        ],
        compiler_params=pltpu.CompilerParams(vmem_limit_bytes=VMEM_LIMIT),
    )(rest_rows, last, cols, x, flat)
    return out.reshape(rhs.shape)


def on_device(rhs, panels, inverses):
    row_index = lax.axis_index("row")
    col_index = lax.axis_index("col")
    row_count = lax.axis_size("row")
    col_count = lax.axis_size("col")
    blocks_here = panels.shape[1]
    col_blocks = rhs.shape[3]
    size = rhs.shape[-1]
    last = lax.all_gather(panels[:, blocks_here - 1, 0], "col", axis=1, tiled=True)
    rest_here, last = lax.optimization_barrier((panels[:, : blocks_here - 1, 0], last))
    rest = lax.all_gather(rest_here, "col", axis=2, tiled=True)
    rhs_last = rhs[blocks_here - 1, 0, :, col_blocks - 1, 0, :]
    upper, lower, g = share_corner(last, rhs_last, row_count, col_count)
    x = solve(upper, lower, g, inverses)
    chosen = []
    for b in range(col_blocks):
        place = col_index // row_count + b * (col_count // row_count)
        from_rest = lax.dynamic_index_in_dim(
            rest, jnp.minimum(place, blocks_here - 2), 1, False
        )
        chosen.append(jnp.where(place == blocks_here - 1, last, from_rest))
    cols = share_columns(jnp.stack(chosen, 1), row_count)
    new_rhs = update(rest, last, cols, x, rhs)
    rows_part = size // row_count
    cols_part = size // col_count
    solved = lax.dynamic_slice(
        x, (0, row_index * rows_part, col_index * cols_part), (2, rows_part, cols_part)
    )
    return (new_rhs, solved)


def solution(mesh):
    in_specs = (P(None, "row", None, None, "col", None), P(None, None, "row", "col", None), P())
    out_specs = (P(None, "row", None, None, "col", None), P(None, "row", "col"))
    return jax.shard_map(
        on_device, mesh=mesh, in_specs=in_specs, out_specs=out_specs, check_vma=False
    )
```

time: 666 us -> 331 us (0.50)
  the two profiles are of different devices: /device:TPU:18 before, /device:TPU:16 now
where the time goes in v1:
time: 331 us
  Pallas kernels  272 us (82%)
  waiting for transfers between devices  28.9 us (9%)
  between operations  14.1 us (4%)
  local copies, waits for them, and re-layouts  12.6 us (4%)
    pallas_call x1, Pallas kernels, share_columns(): pl.pallas_call(functools.partial(column_kernel, row_count), out_shape=jax...  130 us
    pallas_call x1, Pallas kernels, share_corner(): pl.pallas_call(functools.partial(corner_kernel, row_count, col_count), ou...  95.2 us
    all_gather x1, waiting for transfers between devices, on_device(): lax.all_gather(panels[:, blocks_here - 1, 0], 'col', axis=1, tiled=True)  28.8 us
    pallas_call x1, Pallas kernels, solve(): pl.pallas_call(solve_kernel, out_shape=jax.ShapeDtypeStruct((2, size, siz...  25.3 us
    pallas_call x1, Pallas kernels, update(): pl.pallas_call(functools.partial(update_kernel, rest_steps), grid=(steps,...  21.8 us
  transfers between devices with their start and end apart: 2, of which 1 were waited for; matrix products, arithmetic and copies ran while one was open for 2% of the time, Pallas kernels for 36%

profile of v1, /device:TPU:16, one launch (start us, length us, event | category | flops | bytes accessed | tf_op | source)
XLA Modules:
  0.0 330.8 jit_solution(10859164937038649058)
XLA Ops:
  7.2 0.0 all-gather.6.cloned.1.call-start
  7.2 1.7 slice_bitcast_fusion.1
  8.9 0.0 all-gather.6.cloned.1.call-update
  8.9 0.0 all-gather.4.cloned.1.call-start
  9.0 2.1 slice_bitcast_fusion
  11.1 28.8 %all-gather.6.cloned.1.call-done = bf16[2,1,1,512,1024]{4,3,0,2,1:T(8,128)(2,1)} async-done(((bf16[2,1,1,64,1024]{4,3,0,2,1:T(8,128)(2,1)}), bf16[2,1,1,512,1024]{4,3,0,2,1:T(8,128)(2,1)}) %all-gather.6.cloned.1.call-update) | async-done | bytes 2097168 | tf_op jit(solution)/shard_map/all_gather | solution.py:424
  39.9 0.0 all-gather.4.cloned.1.call-update
  39.9 1.9 slice.11
  41.9 1.0 copy.13
  42.9 95.2 %shard_map.51 = (bf16[2,512,1024]{2,1,0:T(8,128)(2,1)}, bf16[2,512,512]{2,1,0:T(8,128)(2,1)}, f32[2,512,512]{2,1,0:T(8,128)}) custom-call(bf16[2,512,1024]{2,1,0:T(8,128)(2,1)} %bitcast.23, f32[512,512]{1,0:T(8,128)} %bitcast.29), custom_call_target="tpu_custom_call" | custom-call | bytes 60000000 | tf_op jit(solution)/shard_map/pallas_call | solution.py:164
  138.2 0.0 copy-start.2
  138.2 1.2 copy-done.2
  139.4 0.0 copy-start
  139.4 25.3 %shard_map.52.x_ref = f32[2,512,512]{2,1,0:T(8,128)S(1)} custom-call(bf16[2,512,1024]{2,1,0:T(8,128)(2,1)} %get-tuple-element.9.upper, bf16[2,512,512]{2,1,0:T(8,128)(2,1)S(1)} %copy-done.2, f32[2,512,512]{2,1,0:T(8,128)} %get-tuple-element.11.g, f32[3,512,512]{2,1,0:T(8,128)} %inverses.1), custom_call_target="tpu_custom_call" | custom-call | flops 13421772800 | bytes 100000000 | tf_op jit(solution)/shard_map/pallas_call | solution.py:267
  164.7 0.0 copy-start.1
  164.7 1.3 copy-done.1
  166.1 0.1 constant_dynamic-slice_fusion
  166.2 0.7 copy.9
  166.9 0.0 all-gather.4.cloned.1.call-done
  166.9 0.0 copy-done
  166.9 2.6 fusion.1
  169.5 0.4 pad_maximum_fusion
  169.8 2.5 copy.6.chosen
  172.3 129.9 %shard_map.50.cols_ref = bf16[2,2,512,1024]{3,2,1,0:T(8,128)(2,1)} custom-call(bf16[2,2,512,1024]{3,2,1,0:T(8,128)(2,1)} %copy.6.chosen), custom_call_target="tpu_custom_call" | custom-call | bytes 60000000 | tf_op jit(solution)/shard_map/pallas_call | solution.py:335
  302.2 21.8 %shard_map.53 = f32[16384,128]{1,0:T(8,128)} custom-call(bf16[2,1536,1024]{2,1,0:T(8,128)(2,1)} %bitcast.26, bf16[2,512,1024]{2,1,0:T(8,128)(2,1)S(1)} %bitcast.25, bf16[2,2,512,1024]{3,2,1,0:T(8,128)(2,1)} %shard_map.50.cols_ref, f32[2,512,512]{2,1,0:T(8,128)} %copy-done.1, f32[16384,128]{1,0:T(8,128)} %bitcast.27), custom_call_target="tpu_custom_call" | custom-call | tf_op jit(solution)/shard_map/pallas_call | solution.py:394
Async XLA Ops:
  7.2 32.7 %all-gather.6.cloned.1.call-start = ((), (), s32[]{:S(2)}) async-start(), calls=%async_computation.1 | async-start | bytes 2359296 | tf_op jit(solution)/shard_map/all_gather | solution.py:424
  8.9 158.0 %all-gather.4.cloned.1.call-start = ((), (), s32[]{:S(2)}) async-start(), calls=%async_computation | async-start | bytes 7077888 | tf_op jit(solution)/shard_map/all_gather | solution.py:426
  138.2 1.2 copy-start.2
  139.4 27.5 %copy-start = (bf16[2,1,1,512,1024]{4,3,0,2,1:T(8,128)(2,1)S(1)}, bf16[2,1,1,512,1024]{4,3,0,2,1:T(8,128)(2,1)}, u32[]{:S(2)}) copy-start(bf16[2,1,1,512,1024]{4,3,0,2,1:T(8,128)(2,1)} %all-gather.6.cloned.1.call-done) | copy-start | bytes 6291460
  164.7 1.3 copy-start.1
Sparse Core Ops, SparseCore 0:
  10.2 29.6 all-gather.5
  41.5 70.6 all-gather.3

commit v2 on v1

--- a/solution.py
+++ b/solution.py
@@ -10,6 +10,7 @@
 SWEEPS = 3
 LANES = 128
 MESH = pl.DeviceIdType.MESH
+WINDOW = 2
 VMEM_LIMIT = 50 * 1024 * 1024
 
 
@@ -27,66 +28,53 @@
     pl.semaphore_wait(barrier, len(partners))
 
 
-def corner_kernel(
-    row_count, col_count, last_ref, g_ref, upper, lower, g_out,
-    send_upper, send_lower, send_sibling, send_g1, send_g2, send_g3, send_g4,
-    recv_corner, recv_sibling, recv_g1, recv_g2, recv_g3, recv_g4, local_sem,
+def other_rows_of(row, row_count):
+    return [lax.rem(row + j, row_count) for j in range(1, row_count)]
+
+
+def g_kernel(
+    row_count, col_count, g_ref, g_out,
+    send_g1, send_g2, send_g3, send_g4, recv_g1, recv_g2, recv_g3, recv_g4, local_sem,
 ):
     row = lax.axis_index("row")
     col = lax.axis_index("col")
     core = lax.rem(col, 2)
     sibling = col + 1 - 2 * core
-    size = g_ref.shape[0]
-    half = size // 2
-    part = size // row_count
+    part = g_ref.shape[0] // row_count
     last_col = col_count - 1
-    other_rows = [lax.rem(row + j, row_count) for j in range(1, row_count)]
+    other_rows = other_rows_of(row, row_count)
     other_cols = [lax.rem(col + 2 * j, col_count) for j in range(1, col_count // 2)]
     greet([(r, col) for r in other_rows] + [(row, c) for c in other_cols] + [(row, sibling)])
 
-    here = pl.ds(pl.multiple_of(core * half, half), half)
-    there = pl.ds(pl.multiple_of((1 - core) * half, half), half)
-
     def rows_of(index):
         return pl.ds(pl.multiple_of(index * part, part), part)
 
-    corners = (
-        (row_count - 2, last_ref.at[:, here, :], upper, send_upper, 0),
-        (row_count - 1, last_ref.at[:, here, pl.ds(size, size)], lower, send_lower, 1),
-    )
-    for source_row, src, out, send, slot in corners:
-        dst = out.at[:, here, :]
-
-        @pl.when(row == source_row)
-        def _():
-            pltpu.make_async_copy(src, dst, local_sem.at[slot]).start()
-            for j, r in enumerate(other_rows):
-                remote(src, dst, send.at[j], recv_corner.at[slot], r, col).start()
-
-        @pl.when(jnp.logical_and(row == source_row, col == last_col))
-        def _():
-            mine = rows_of(row)
-            pltpu.make_async_copy(
-                g_ref.at[mine, :], g_out.at[slot, mine, :], local_sem.at[2 + slot]
-            ).start()
-            for j, r in enumerate(other_rows):
-                theirs = rows_of(r)
-                remote(
-                    g_ref.at[theirs, :], g_out.at[slot, theirs, :],
-                    send_g1.at[slot, j], recv_g1.at[slot], r, col,
-                ).start()
-
     mine = rows_of(row)
     g_mine = g_out.at[:, mine, :]
+    sources = ((row_count - 2, 0), (row_count - 1, 1))
 
     @pl.when(col == last_col)
     def _():
-        for source_row, src, out, send, slot in corners:
+        for source_row, slot in sources:
+
+            @pl.when(row == source_row)
+            def _():
+                pltpu.make_async_copy(
+                    g_ref.at[mine, :], g_out.at[slot, mine, :], local_sem.at[slot]
+                ).start()
+                for j, r in enumerate(other_rows):
+                    theirs = rows_of(r)
+                    remote(
+                        g_ref.at[theirs, :], g_out.at[slot, theirs, :],
+                        send_g1.at[slot, j], recv_g1.at[slot], r, col,
+                    ).start()
+
+        for source_row, slot in sources:
             piece = g_out.at[slot, mine, :]
 
             @pl.when(row == source_row)
             def _():
-                pltpu.make_async_copy(g_ref.at[mine, :], piece, local_sem.at[2 + slot]).wait()
+                pltpu.make_async_copy(g_ref.at[mine, :], piece, local_sem.at[slot]).wait()
 
             @pl.when(row != source_row)
             def _():
@@ -94,19 +82,6 @@
 
         for j, c in enumerate(other_cols):
             remote(g_mine, g_mine, send_g2.at[j], recv_g2, row, c).start()
-
-    for source_row, src, out, send, slot in corners:
-        dst = out.at[:, here, :]
-
-        @pl.when(row == source_row)
-        def _():
-            pltpu.make_async_copy(src, dst, local_sem.at[slot]).wait()
-
-        @pl.when(row != source_row)
-        def _():
-            remote(dst, dst, send.at[0], recv_corner.at[slot], row, col).wait_recv()
-
-        remote(dst, dst, send_sibling.at[slot], recv_sibling.at[slot], row, sibling).start()
 
     @pl.when(core == 1)
     def _():
@@ -116,68 +91,194 @@
 
         for j, r in enumerate(other_rows):
             remote(g_mine, g_mine, send_g3.at[j], recv_g3.at[row], r, col).start()
+        remote(g_mine, g_mine, send_g4.at[row], recv_g4.at[row], row, sibling).start()
         for r in other_rows:
             piece = g_out.at[:, rows_of(r), :]
             remote(piece, piece, send_g3.at[0], recv_g3.at[r], row, col).wait_recv()
-        remote(g_out, g_out, send_g4, recv_g4, row, sibling).start()
-
-    @pl.when(core == 0)
-    def _():
-        remote(g_out, g_out, send_g4, recv_g4, row, sibling).wait_recv()
-
-    for source_row, src, out, send, slot in corners:
-        dst = out.at[:, here, :]
-        arriving = out.at[:, there, :]
-        remote(arriving, arriving, send_sibling.at[slot], recv_sibling.at[slot], row, sibling).wait_recv()
-        remote(dst, dst, send_sibling.at[slot], recv_sibling.at[slot], row, sibling).wait_send()
-
-        @pl.when(row == source_row)
+            remote(piece, piece, send_g4.at[r], recv_g4.at[r], row, sibling).start()
+
+    for r in [row] + other_rows:
+        piece = g_out.at[:, rows_of(r), :]
+
+        @pl.when(core == 0)
         def _():
-            for j, r in enumerate(other_rows):
-                remote(src, dst, send.at[j], recv_corner.at[slot], r, col).wait_send()
-
-        @pl.when(jnp.logical_and(row == source_row, col == last_col))
+            remote(piece, piece, send_g4.at[r], recv_g4.at[r], row, sibling).wait_recv()
+
+        @pl.when(core == 1)
         def _():
-            for j, r in enumerate(other_rows):
-                theirs = rows_of(r)
-                remote(
-                    g_ref.at[theirs, :], g_out.at[slot, theirs, :],
-                    send_g1.at[slot, j], recv_g1.at[slot], r, col,
-                ).wait_send()
+            remote(piece, piece, send_g4.at[r], recv_g4.at[r], row, sibling).wait_send()
+
+    @pl.when(core == 1)
+    def _():
+        for j, r in enumerate(other_rows):
+            remote(g_mine, g_mine, send_g3.at[j], recv_g3.at[row], r, col).wait_send()
 
     @pl.when(col == last_col)
     def _():
+        for source_row, slot in sources:
+
+            @pl.when(row == source_row)
+            def _():
+                for j, r in enumerate(other_rows):
+                    theirs = rows_of(r)
+                    remote(
+                        g_ref.at[theirs, :], g_out.at[slot, theirs, :],
+                        send_g1.at[slot, j], recv_g1.at[slot], r, col,
+                    ).wait_send()
+
         for j, c in enumerate(other_cols):
             remote(g_mine, g_mine, send_g2.at[j], recv_g2, row, c).wait_send()
 
-    @pl.when(core == 1)
-    def _():
-        for j, r in enumerate(other_rows):
-            remote(g_mine, g_mine, send_g3.at[j], recv_g3.at[row], r, col).wait_send()
-        remote(g_out, g_out, send_g4, recv_g4, row, sibling).wait_send()
-
-
-def share_corner(last_rows, rhs_last, row_count, col_count):
+
+def share_g(rhs_last, row_count, col_count):
     size = rhs_last.shape[0]
     dma = pltpu.SemaphoreType.DMA
     peers = row_count - 1
     return pl.pallas_call(
-        functools.partial(corner_kernel, row_count, col_count),
-        out_shape=(
-            jax.ShapeDtypeStruct((2, size, 2 * size), jnp.bfloat16),
-            jax.ShapeDtypeStruct((2, size, size), jnp.bfloat16),
-            jax.ShapeDtypeStruct((2, size, size), jnp.float32),
-        ),
-        in_specs=[pl.BlockSpec(memory_space=pl.ANY)] * 2,
-        out_specs=[pl.BlockSpec(memory_space=pl.ANY)] * 3,
+        functools.partial(g_kernel, row_count, col_count),
+        out_shape=jax.ShapeDtypeStruct((2, size, size), jnp.float32),
+        in_specs=[pl.BlockSpec(memory_space=pl.ANY)],
+        out_specs=pl.BlockSpec(memory_space=pl.ANY),
         scratch_shapes=[
-            dma((peers,)), dma((peers,)), dma((2,)), dma((2, peers)),
-            dma((col_count // 2,)), dma((peers,)), dma,
-            dma((2,)), dma((2,)), dma((2,)), dma, dma((row_count,)), dma, dma((4,)),
+            dma((2, peers)), dma((col_count // 2,)), dma((peers,)), dma((row_count,)),
+            dma((2,)), dma, dma((row_count,)), dma((row_count,)), dma((2,)),
         ],
         compiler_params=pltpu.CompilerParams(collective_id=0, has_side_effects=True),
         cost_estimate=pl.CostEstimate(flops=0, bytes_accessed=60_000_000, transcendentals=0),
-    )(last_rows, rhs_last)
+    )(rhs_last)
+
+
+def chain_of(row, source, backward, row_count):
+    place = jnp.int32(0)
+    after = jnp.int32(0)
+    for s in range(row_count):
+        forward = [s ^ (i ^ (i >> 1)) for i in range(row_count)]
+        for b, order in enumerate((forward, forward[:1] + forward[:0:-1])):
+            for i, r in enumerate(order):
+                hit = jnp.logical_and(jnp.logical_and(source == s, backward == b), row == r)
+                place = jnp.where(hit, i, place)
+                after = jnp.where(hit, order[(i + 1) % row_count], after)
+    return place, after
+
+
+def run_chains(chains, row, col, row_count, on_arrival):
+    for n in range(max(len(chain[2]) for chain in chains)):
+        for which, (place, after, chunks, send, recv) in enumerate(chains):
+            if n >= len(chunks):
+                continue
+            src, dst = chunks[n]
+
+            @pl.when(place == 0)
+            def _():
+                if n >= WINDOW:
+                    old_src, old_dst = chunks[n - WINDOW]
+                    remote(
+                        old_src, old_dst, send.at[n - WINDOW], recv.at[n - WINDOW], after, col
+                    ).wait_send()
+                remote(src, dst, send.at[n], recv.at[n], after, col).start()
+
+            @pl.when(place > 0)
+            def _():
+                remote(dst, dst, send.at[n], recv.at[n], after, col).wait_recv()
+
+                @pl.when(place < row_count - 1)
+                def _():
+                    remote(dst, dst, send.at[n], recv.at[n], after, col).start()
+
+                on_arrival(which, n)
+
+    for place, after, chunks, send, recv in chains:
+        for n, (src, dst) in enumerate(chunks):
+            waits = place < row_count - 1
+            if n < len(chunks) - WINDOW:
+                waits = jnp.logical_and(waits, place > 0)
+
+            @pl.when(waits)
+            def _():
+                remote(dst, dst, send.at[n], recv.at[n], after, col).wait_send()
+
+
+def corner_kernel(
+    row_count, last_ref, upper, lower,
+    send_upper, recv_upper, send_lower, recv_lower,
+    sib_send_upper, sib_recv_upper, sib_send_lower, sib_recv_lower, local_sem,
+):
+    row = lax.axis_index("row")
+    col = lax.axis_index("col")
+    core = lax.rem(col, 2)
+    sibling = col + 1 - 2 * core
+    size = last_ref.shape[1]
+    half = size // 2
+    part = half // 4
+    greet([(r, col) for r in other_rows_of(row, row_count)] + [(row, sibling)])
+
+    own_copies = (
+        (row_count - 2, last_ref, upper, local_sem.at[0]),
+        (row_count - 1, last_ref.at[:, :, pl.ds(size, size)], lower, local_sem.at[1]),
+    )
+    for source_row, src, out, sem in own_copies:
+
+        @pl.when(row == source_row)
+        def _():
+            pltpu.make_async_copy(src, out, sem).start()
+
+    def rows_at(which_half, p):
+        return pl.ds(pl.multiple_of(which_half * half + p * part, part), part)
+
+    chains = []
+    siblings = []
+    for source_row, src, out, sends in (
+        (row_count - 2, last_ref, upper, (send_upper, recv_upper, sib_send_upper, sib_recv_upper)),
+        (row_count - 1, last_ref.at[:, :, pl.ds(size, size)], lower,
+         (send_lower, recv_lower, sib_send_lower, sib_recv_lower)),
+    ):
+        place, after = chain_of(row, source_row, core, row_count)
+        pieces = [(m, p) for p in range(4) for m in range(2)]
+        chunks = [
+            (src.at[m, rows_at(core, p), :], out.at[m, rows_at(core, p), :]) for m, p in pieces
+        ]
+        arriving = [out.at[m, rows_at(1 - core, p), :] for m, p in pieces]
+        chains.append((place, after, chunks, sends[0], sends[1]))
+        siblings.append((place, arriving, sends[2], sends[3]))
+
+    def to_sibling(which, n):
+        dst = chains[which][2][n][1]
+        _, _, send, recv = siblings[which]
+        remote(dst, dst, send.at[n], recv.at[n], row, sibling).start()
+
+    run_chains(chains, row, col, row_count, to_sibling)
+
+    for which, (place, arriving, send, recv) in enumerate(siblings):
+
+        @pl.when(place > 0)
+        def _():
+            for n, ref in enumerate(arriving):
+                dst = chains[which][2][n][1]
+                remote(ref, ref, send.at[n], recv.at[n], row, sibling).wait_recv()
+                remote(dst, dst, send.at[n], recv.at[n], row, sibling).wait_send()
+
+    for source_row, src, out, sem in own_copies:
+
+        @pl.when(row == source_row)
+        def _():
+            pltpu.make_async_copy(src, out, sem).wait()
+
+
+def share_corner(last_rows, row_count):
+    _, size, width = last_rows.shape
+    dma = pltpu.SemaphoreType.DMA
+    return pl.pallas_call(
+        functools.partial(corner_kernel, row_count),
+        out_shape=(
+            jax.ShapeDtypeStruct((2, size, width), jnp.bfloat16),
+            jax.ShapeDtypeStruct((2, size, size), jnp.bfloat16),
+        ),
+        in_specs=[pl.BlockSpec(memory_space=pl.ANY)],
+        out_specs=[pl.BlockSpec(memory_space=pl.ANY)] * 2,
+        scratch_shapes=[dma((8,))] * 8 + [dma((2,))],
+        compiler_params=pltpu.CompilerParams(collective_id=2, has_side_effects=True),
+        cost_estimate=pl.CostEstimate(flops=0, bytes_accessed=60_000_000, transcendentals=0),
+    )(last_rows)
 
 
 def mm(left, right):
@@ -280,53 +381,29 @@
     )(upper, lower, g, inverses)
 
 
-def gray(index):
-    return index ^ (index >> 1)
-
-
 def column_kernel(row_count, chosen, out, send, recv, local_sem):
     row = lax.axis_index("row")
     col = lax.axis_index("col")
-    source = lax.rem(col, row_count)
     matrices, blocks, size, _ = chosen.shape
     part = size // 4
-    chunks = [
-        (m, b, pl.ds(p * part, part)) for b in range(blocks) for p in range(4) for m in range(matrices)
-    ]
-    places = [gray(i) for i in range(row_count)]
-
-    def at_place(place):
-        value = jnp.int32(0)
-        for s in range(row_count):
-            value = jnp.where(source == s, s ^ places[place], value)
-        return value
-
-    chain = [at_place(i) for i in range(row_count)]
-    barrier = pltpu.get_barrier_semaphore()
-    for i in range(row_count):
-
-        @pl.when(row == chain[i])
-        def _():
-            around = [chain[j] for j in (i - 1, i + 1) if 0 <= j < row_count]
-            for r in around:
-                pl.semaphore_signal(barrier, inc=1, device_id=(r, col), device_id_type=MESH)
-            pl.semaphore_wait(barrier, len(around))
-            if i == 0:
-                pltpu.make_async_copy(chosen, out, local_sem).start()
-            for n, (m, b, rows) in enumerate(chunks):
-                dst = out.at[m, b, rows, :]
-                src = chosen.at[m, b, rows, :] if i == 0 else dst
-                if i > 0:
-                    remote(dst, dst, send.at[n], recv.at[n], row, col).wait_recv()
-                if i < row_count - 1:
-                    remote(src, dst, send.at[n], recv.at[n], chain[i + 1], col).start()
-            if i == 0:
-                pltpu.make_async_copy(chosen, out, local_sem).wait()
-            if i < row_count - 1:
-                for n, (m, b, rows) in enumerate(chunks):
-                    dst = out.at[m, b, rows, :]
-                    src = chosen.at[m, b, rows, :] if i == 0 else dst
-                    remote(src, dst, send.at[n], recv.at[n], chain[i + 1], col).wait_send()
+    greet([(r, col) for r in other_rows_of(row, row_count)])
+    place, after = chain_of(row, lax.rem(col, row_count), 0, row_count)
+
+    @pl.when(place == 0)
+    def _():
+        pltpu.make_async_copy(chosen, out, local_sem).start()
+
+    chunks = []
+    for b in range(blocks):
+        for p in range(4):
+            for m in range(matrices):
+                rows = pl.ds(p * part, part)
+                chunks.append((chosen.at[m, b, rows, :], out.at[m, b, rows, :]))
+    run_chains([(place, after, chunks, send, recv)], row, col, row_count, lambda which, n: None)
+
+    @pl.when(place == 0)
+    def _():
+        pltpu.make_async_copy(chosen, out, local_sem).wait()
 
 
 def share_columns(chosen, row_count):
@@ -422,10 +499,11 @@
     col_blocks = rhs.shape[3]
     size = rhs.shape[-1]
     last = lax.all_gather(panels[:, blocks_here - 1, 0], "col", axis=1, tiled=True)
-    rest_here, last = lax.optimization_barrier((panels[:, : blocks_here - 1, 0], last))
+    rhs_last = rhs[blocks_here - 1, 0, :, col_blocks - 1, 0, :]
+    g = share_g(rhs_last, row_count, col_count)
+    rest_here, last, g = lax.optimization_barrier((panels[:, : blocks_here - 1, 0], last, g))
     rest = lax.all_gather(rest_here, "col", axis=2, tiled=True)
-    rhs_last = rhs[blocks_here - 1, 0, :, col_blocks - 1, 0, :]
-    upper, lower, g = share_corner(last, rhs_last, row_count, col_count)
+    upper, lower = share_corner(last, row_count)
     x = solve(upper, lower, g, inverses)
     chosen = []
     for b in range(col_blocks):

time: 331 us -> 420 us (1.27)
  the two profiles are of different devices: /device:TPU:16 before, /device:TPU:19 now
where the time goes in v2:
time: 420 us
  Pallas kernels  391 us (93%)
  between operations  14.2 us (3%)
  local copies, waits for them, and re-layouts  11.4 us (3%)
    pallas_call x1, Pallas kernels, share_corner(): pl.pallas_call(functools.partial(corner_kernel, row_count), out_shape=(ja...  150 us
    pallas_call x1, Pallas kernels, share_columns(): pl.pallas_call(functools.partial(column_kernel, row_count), out_shape=jax...  135 us
    pallas_call x1, Pallas kernels, share_g(): pl.pallas_call(functools.partial(g_kernel, row_count, col_count), out_sha...  60.1 us
    pallas_call x1, Pallas kernels, solve(): pl.pallas_call(solve_kernel, out_shape=jax.ShapeDtypeStruct((2, size, siz...  25.3 us
    pallas_call x1, Pallas kernels, update(): pl.pallas_call(functools.partial(update_kernel, rest_steps), grid=(steps,...  21.8 us
  transfers between devices with their start and end apart: 2, of which 0 were waited for; matrix products, arithmetic and copies ran while one was open for 1% of the time, Pallas kernels for 56%

profile of v2, /device:TPU:19, one launch (start us, length us, event | category | flops | bytes accessed | tf_op | source)
XLA Modules:
  0.0 420.0 jit_solution(13889930708984027218)
XLA Ops:
  7.2 0.0 all-gather.6.cloned.1.call-start
  7.2 1.7 slice_bitcast_fusion.1
  8.9 0.0 all-gather.6.cloned.1.call-update
  8.9 0.0 all-gather.4.cloned.1.call-start
  9.0 1.9 slice.11
  10.9 1.0 copy.13
  12.0 0.0 copy-start.3
  12.0 60.1 %shard_map.50.g = f32[2,512,512]{2,1,0:T(8,128)} custom-call(f32[512,512]{1,0:T(8,128)} %bitcast.29), custom_call_target="tpu_custom_call" | custom-call | bytes 60000000 | tf_op jit(solution)/shard_map/pallas_call | solution.py:137
  72.1 0.0 copy-done.3
  72.1 0.9 slice_bitcast_fusion
  73.0 0.0 all-gather.6.cloned.1.call-done
  73.0 0.0 all-gather.4.cloned.1.call-update
  73.1 149.6 %shard_map.52 = (bf16[2,512,1024]{2,1,0:T(8,128)(2,1)}, bf16[2,512,512]{2,1,0:T(8,128)(2,1)}) custom-call(bf16[2,512,1024]{2,1,0:T(8,128)(2,1)} %bitcast.23), custom_call_target="tpu_custom_call" | custom-call | bytes 60000000 | tf_op jit(solution)/shard_map/pallas_call | solution.py:270
  222.7 0.0 copy-start.2
  222.7 1.2 copy-done.2
  223.9 0.0 copy-start
  223.9 25.3 %shard_map.53.x_ref = f32[2,512,512]{2,1,0:T(8,128)S(1)} custom-call(bf16[2,512,1024]{2,1,0:T(8,128)(2,1)} %get-tuple-element.9.upper, bf16[2,512,512]{2,1,0:T(8,128)(2,1)S(1)} %copy-done.2, f32[2,512,512]{2,1,0:T(8,128)} %shard_map.50.g, f32[3,512,512]{2,1,0:T(8,128)} %inverses.1), custom_call_target="tpu_custom_call" | custom-call | flops 13421772800 | bytes 100000000 | tf_op jit(solution)/shard_map/pallas_call | solution.py:368
  249.3 0.0 copy-start.1
  249.3 1.3 copy-done.1
  250.6 0.1 constant_dynamic-slice_fusion
  250.7 0.7 copy.9
  251.4 0.0 all-gather.4.cloned.1.call-done
  251.4 0.0 copy-done
  251.4 2.6 fusion.1
  254.0 0.4 pad_maximum_fusion
  254.4 2.5 copy.7.chosen
  256.8 134.6 %shard_map.51.cols_ref = bf16[2,2,512,1024]{3,2,1,0:T(8,128)(2,1)} custom-call(bf16[2,2,512,1024]{3,2,1,0:T(8,128)(2,1)} %copy.7.chosen), custom_call_target="tpu_custom_call" | custom-call | bytes 60000000 | tf_op jit(solution)/shard_map/pallas_call | solution.py:412
  391.4 21.8 %shard_map.54 = f32[16384,128]{1,0:T(8,128)} custom-call(bf16[2,1536,1024]{2,1,0:T(8,128)(2,1)} %bitcast.26, bf16[2,512,1024]{2,1,0:T(8,128)(2,1)S(1)} %bitcast.25, bf16[2,2,512,1024]{3,2,1,0:T(8,128)(2,1)} %shard_map.51.cols_ref, f32[2,512,512]{2,1,0:T(8,128)} %copy-done.1, f32[16384,128]{1,0:T(8,128)} %bitcast.27), custom_call_target="tpu_custom_call" | custom-call | tf_op jit(solution)/shard_map/pallas_call | solution.py:471
Async XLA Ops:
  7.2 65.9 %all-gather.6.cloned.1.call-start = ((), (), s32[]{:S(2)}) async-start(), calls=%async_computation.1 | async-start | bytes 2359296 | tf_op jit(solution)/shard_map/all_gather | solution.py:501
  8.9 242.5 %all-gather.4.cloned.1.call-start = ((), (), s32[]{:S(2)}) async-start(), calls=%async_computation | async-start | bytes 7077888 | tf_op jit(solution)/shard_map/all_gather | solution.py:505
  12.0 60.1 %copy-start.3 = (bf16[2,4,1,64,1024]{4,3,2,1,0:T(8,128)(2,1)S(1)}, bf16[2,4,1,64,1024]{4,3,2,1,0:T(8,128)(2,1)}, u32[]{:S(2)}) copy-start(bf16[2,4,1,64,1024]{4,3,2,1,0:T(8,128)(2,1)} %param.4) | copy-start | bytes 3145732
  222.7 1.2 copy-start.2
  223.9 27.5 %copy-start = (bf16[2,1,1,512,1024]{4,3,0,2,1:T(8,128)(2,1)S(1)}, bf16[2,1,1,512,1024]{4,3,0,2,1:T(8,128)(2,1)}, u32[]{:S(2)}) copy-start(bf16[2,1,1,512,1024]{4,3,0,2,1:T(8,128)(2,1)} %all-gather.6.cloned.1.call-done) | copy-start | bytes 6291460
  249.3 1.3 copy-start.1
Sparse Core Ops, SparseCore 0:
  9.6 37.0 all-gather.5
  73.2 62.5 all-gather.3

commit v3 on v2

--- a/solution.py
+++ b/solution.py
@@ -10,7 +10,8 @@
 SWEEPS = 3
 LANES = 128
 MESH = pl.DeviceIdType.MESH
-WINDOW = 2
+CORNER_PARTS = 4
+COLUMN_PARTS = 4
 VMEM_LIMIT = 50 * 1024 * 1024
 
 
@@ -34,100 +35,98 @@
 
 def g_kernel(
     row_count, col_count, g_ref, g_out,
-    send_g1, send_g2, send_g3, send_g4, recv_g1, recv_g2, recv_g3, recv_g4, local_sem,
+    send_first, send_line, send_rows, send_sibling,
+    recv_first, recv_line, recv_rows, recv_sibling, local_sem,
 ):
     row = lax.axis_index("row")
     col = lax.axis_index("col")
     core = lax.rem(col, 2)
     sibling = col + 1 - 2 * core
-    part = g_ref.shape[0] // row_count
+    part = g_ref.shape[0] // (2 * row_count)
     last_col = col_count - 1
     other_rows = other_rows_of(row, row_count)
     other_cols = [lax.rem(col + 2 * j, col_count) for j in range(1, col_count // 2)]
-    greet([(r, col) for r in other_rows] + [(row, c) for c in other_cols] + [(row, sibling)])
-
-    def rows_of(index):
-        return pl.ds(pl.multiple_of(index * part, part), part)
-
-    mine = rows_of(row)
+    on_last_chip = col >= last_col - 1
+    greet(
+        [(r, col) for r in other_rows]
+        + [(r, sibling) for r in other_rows]
+        + [(row, c) for c in other_cols]
+        + [(row, sibling)]
+    )
+
+    def rows_of(r, k):
+        return pl.ds(pl.multiple_of((2 * r + k) * part, part), part)
+
+    mine = rows_of(row, core)
     g_mine = g_out.at[:, mine, :]
     sources = ((row_count - 2, 0), (row_count - 1, 1))
 
-    @pl.when(col == last_col)
+    def first_sends(slot):
+        for j, (r, k) in enumerate(
+            [(r, k) for r in other_rows for k in range(2)] + [(row, 0)]
+        ):
+            theirs = rows_of(r, k)
+            yield remote(
+                g_ref.at[theirs, :], g_out.at[slot, theirs, :],
+                send_first.at[slot, j], recv_first.at[slot], r, last_col - 1 + k,
+            )
+
+    @pl.when(on_last_chip)
     def _():
         for source_row, slot in sources:
 
-            @pl.when(row == source_row)
+            @pl.when(jnp.logical_and(row == source_row, col == last_col))
             def _():
                 pltpu.make_async_copy(
                     g_ref.at[mine, :], g_out.at[slot, mine, :], local_sem.at[slot]
                 ).start()
-                for j, r in enumerate(other_rows):
-                    theirs = rows_of(r)
-                    remote(
-                        g_ref.at[theirs, :], g_out.at[slot, theirs, :],
-                        send_g1.at[slot, j], recv_g1.at[slot], r, col,
-                    ).start()
+                for copy in first_sends(slot):
+                    copy.start()
 
         for source_row, slot in sources:
             piece = g_out.at[slot, mine, :]
-
-            @pl.when(row == source_row)
+            holder = jnp.logical_and(row == source_row, col == last_col)
+
+            @pl.when(holder)
             def _():
                 pltpu.make_async_copy(g_ref.at[mine, :], piece, local_sem.at[slot]).wait()
 
-            @pl.when(row != source_row)
-            def _():
-                remote(piece, piece, send_g1.at[slot, 0], recv_g1.at[slot], row, col).wait_recv()
+            @pl.when(jnp.logical_not(holder))
+            def _():
+                remote(piece, piece, send_first.at[slot, 0], recv_first.at[slot], row, col).wait_recv()
 
         for j, c in enumerate(other_cols):
-            remote(g_mine, g_mine, send_g2.at[j], recv_g2, row, c).start()
-
-    @pl.when(core == 1)
-    def _():
-        @pl.when(col != last_col)
-        def _():
-            remote(g_mine, g_mine, send_g2.at[0], recv_g2, row, col).wait_recv()
-
-        for j, r in enumerate(other_rows):
-            remote(g_mine, g_mine, send_g3.at[j], recv_g3.at[row], r, col).start()
-        remote(g_mine, g_mine, send_g4.at[row], recv_g4.at[row], row, sibling).start()
-        for r in other_rows:
-            piece = g_out.at[:, rows_of(r), :]
-            remote(piece, piece, send_g3.at[0], recv_g3.at[r], row, col).wait_recv()
-            remote(piece, piece, send_g4.at[r], recv_g4.at[r], row, sibling).start()
-
+            remote(g_mine, g_mine, send_line.at[j], recv_line, row, c).start()
+
+    @pl.when(jnp.logical_not(on_last_chip))
+    def _():
+        remote(g_mine, g_mine, send_line.at[0], recv_line, row, col).wait_recv()
+
+    for j, r in enumerate(other_rows):
+        remote(g_mine, g_mine, send_rows.at[j], recv_rows.at[row], r, col).start()
+    remote(g_mine, g_mine, send_sibling.at[row], recv_sibling.at[row], row, sibling).start()
+    for r in other_rows:
+        piece = g_out.at[:, rows_of(r, core), :]
+        remote(piece, piece, send_rows.at[0], recv_rows.at[r], row, col).wait_recv()
+        remote(piece, piece, send_sibling.at[r], recv_sibling.at[r], row, sibling).start()
     for r in [row] + other_rows:
-        piece = g_out.at[:, rows_of(r), :]
-
-        @pl.when(core == 0)
-        def _():
-            remote(piece, piece, send_g4.at[r], recv_g4.at[r], row, sibling).wait_recv()
-
-        @pl.when(core == 1)
-        def _():
-            remote(piece, piece, send_g4.at[r], recv_g4.at[r], row, sibling).wait_send()
-
-    @pl.when(core == 1)
-    def _():
-        for j, r in enumerate(other_rows):
-            remote(g_mine, g_mine, send_g3.at[j], recv_g3.at[row], r, col).wait_send()
-
-    @pl.when(col == last_col)
+        piece = g_out.at[:, rows_of(r, 1 - core), :]
+        remote(piece, piece, send_sibling.at[r], recv_sibling.at[r], row, sibling).wait_recv()
+        remote(piece, piece, send_sibling.at[r], recv_sibling.at[r], row, sibling).wait_send()
+    for j, r in enumerate(other_rows):
+        remote(g_mine, g_mine, send_rows.at[j], recv_rows.at[row], r, col).wait_send()
+
+    @pl.when(on_last_chip)
     def _():
         for source_row, slot in sources:
 
-            @pl.when(row == source_row)
-            def _():
-                for j, r in enumerate(other_rows):
-                    theirs = rows_of(r)
-                    remote(
-                        g_ref.at[theirs, :], g_out.at[slot, theirs, :],
-                        send_g1.at[slot, j], recv_g1.at[slot], r, col,
-                    ).wait_send()
+            @pl.when(jnp.logical_and(row == source_row, col == last_col))
+            def _():
+                for copy in first_sends(slot):
+                    copy.wait_send()
 
         for j, c in enumerate(other_cols):
-            remote(g_mine, g_mine, send_g2.at[j], recv_g2, row, c).wait_send()
+            remote(g_mine, g_mine, send_line.at[j], recv_line, row, c).wait_send()
 
 
 def share_g(rhs_last, row_count, col_count):
@@ -140,7 +139,7 @@
         in_specs=[pl.BlockSpec(memory_space=pl.ANY)],
         out_specs=pl.BlockSpec(memory_space=pl.ANY),
         scratch_shapes=[
-            dma((2, peers)), dma((col_count // 2,)), dma((peers,)), dma((row_count,)),
+            dma((2, 2 * peers + 1)), dma((col_count // 2,)), dma((peers,)), dma((row_count,)),
             dma((2,)), dma, dma((row_count,)), dma((row_count,)), dma((2,)),
         ],
         compiler_params=pltpu.CompilerParams(collective_id=0, has_side_effects=True),
@@ -162,20 +161,16 @@
 
 
 def run_chains(chains, row, col, row_count, on_arrival):
-    for n in range(max(len(chain[2]) for chain in chains)):
-        for which, (place, after, chunks, send, recv) in enumerate(chains):
-            if n >= len(chunks):
-                continue
-            src, dst = chunks[n]
+    for n in range(len(chains[0][3])):
+        for place, after, start, landings, send, recv in chains:
 
             @pl.when(place == 0)
             def _():
-                if n >= WINDOW:
-                    old_src, old_dst = chunks[n - WINDOW]
-                    remote(
-                        old_src, old_dst, send.at[n - WINDOW], recv.at[n - WINDOW], after, col
-                    ).wait_send()
-                remote(src, dst, send.at[n], recv.at[n], after, col).start()
+                start(n, after)
+
+    for n in range(len(chains[0][3])):
+        for which, (place, after, start, landings, send, recv) in enumerate(chains):
+            dst = landings[n]
 
             @pl.when(place > 0)
             def _():
@@ -187,21 +182,16 @@
 
                 on_arrival(which, n)
 
-    for place, after, chunks, send, recv in chains:
-        for n, (src, dst) in enumerate(chunks):
-            waits = place < row_count - 1
-            if n < len(chunks) - WINDOW:
-                waits = jnp.logical_and(waits, place > 0)
-
-            @pl.when(waits)
-            def _():
+    for place, after, start, landings, send, recv in chains:
+
+        @pl.when(place < row_count - 1)
+        def _():
+            for n, dst in enumerate(landings):
                 remote(dst, dst, send.at[n], recv.at[n], after, col).wait_send()
 
 
 def corner_kernel(
-    row_count, last_ref, upper, lower,
-    send_upper, recv_upper, send_lower, recv_lower,
-    sib_send_upper, sib_recv_upper, sib_send_lower, sib_recv_lower, local_sem,
+    row_count, last_ref, upper, lower, send, recv, sibling_send, sibling_recv, local_sem
 ):
     row = lax.axis_index("row")
     col = lax.axis_index("col")
@@ -209,59 +199,61 @@
     sibling = col + 1 - 2 * core
     size = last_ref.shape[1]
     half = size // 2
-    part = half // 4
+    part = half // CORNER_PARTS
     greet([(r, col) for r in other_rows_of(row, row_count)] + [(row, sibling)])
-
-    own_copies = (
-        (row_count - 2, last_ref, upper, local_sem.at[0]),
-        (row_count - 1, last_ref.at[:, :, pl.ds(size, size)], lower, local_sem.at[1]),
+    sources = (
+        (row_count - 2, last_ref, upper),
+        (row_count - 1, last_ref.at[:, :, pl.ds(size, size)], lower),
     )
-    for source_row, src, out, sem in own_copies:
+    for slot, (source_row, src, out) in enumerate(sources):
 
         @pl.when(row == source_row)
         def _():
-            pltpu.make_async_copy(src, out, sem).start()
+            pltpu.make_async_copy(src, out, local_sem.at[slot]).start()
 
     def rows_at(which_half, p):
         return pl.ds(pl.multiple_of(which_half * half + p * part, part), part)
 
     chains = []
-    siblings = []
-    for source_row, src, out, sends in (
-        (row_count - 2, last_ref, upper, (send_upper, recv_upper, sib_send_upper, sib_recv_upper)),
-        (row_count - 1, last_ref.at[:, :, pl.ds(size, size)], lower,
-         (send_lower, recv_lower, sib_send_lower, sib_recv_lower)),
-    ):
-        place, after = chain_of(row, source_row, core, row_count)
-        pieces = [(m, p) for p in range(4) for m in range(2)]
-        chunks = [
-            (src.at[m, rows_at(core, p), :], out.at[m, rows_at(core, p), :]) for m, p in pieces
-        ]
-        arriving = [out.at[m, rows_at(1 - core, p), :] for m, p in pieces]
-        chains.append((place, after, chunks, sends[0], sends[1]))
-        siblings.append((place, arriving, sends[2], sends[3]))
+    arriving = []
+    for slot, (source_row, src, out) in enumerate(sources):
+        for way in range(2):
+            index = 2 * slot + way
+            place, after = chain_of(row, source_row, way, row_count)
+
+            def start(n, to, index=index, way=way, src=src, out=out):
+                rows = rows_at(core, n)
+                remote(
+                    src.at[way, rows, :], out.at[way, rows, :],
+                    send.at[index, n], recv.at[index, n], to, col,
+                ).start()
+
+            landings = [out.at[way, rows_at(core, n), :] for n in range(CORNER_PARTS)]
+            arriving.append([out.at[way, rows_at(1 - core, n), :] for n in range(CORNER_PARTS)])
+            chains.append((place, after, start, landings, send.at[index], recv.at[index]))
 
     def to_sibling(which, n):
-        dst = chains[which][2][n][1]
-        _, _, send, recv = siblings[which]
-        remote(dst, dst, send.at[n], recv.at[n], row, sibling).start()
+        dst = chains[which][3][n]
+        remote(dst, dst, sibling_send.at[which, n], sibling_recv.at[which, n], row, sibling).start()
 
     run_chains(chains, row, col, row_count, to_sibling)
 
-    for which, (place, arriving, send, recv) in enumerate(siblings):
-
-        @pl.when(place > 0)
+    for which, chain in enumerate(chains):
+
+        @pl.when(chain[0] > 0)
         def _():
-            for n, ref in enumerate(arriving):
-                dst = chains[which][2][n][1]
-                remote(ref, ref, send.at[n], recv.at[n], row, sibling).wait_recv()
-                remote(dst, dst, send.at[n], recv.at[n], row, sibling).wait_send()
-
-    for source_row, src, out, sem in own_copies:
+            for n, ref in enumerate(arriving[which]):
+                done = remote(
+                    ref, ref, sibling_send.at[which, n], sibling_recv.at[which, n], row, sibling
+                )
+                done.wait_recv()
+                done.wait_send()
+
+    for slot, (source_row, src, out) in enumerate(sources):
 
         @pl.when(row == source_row)
         def _():
-            pltpu.make_async_copy(src, out, sem).wait()
+            pltpu.make_async_copy(src, out, local_sem.at[slot]).wait()
 
 
 def share_corner(last_rows, row_count):
@@ -275,7 +267,7 @@
         ),
         in_specs=[pl.BlockSpec(memory_space=pl.ANY)],
         out_specs=[pl.BlockSpec(memory_space=pl.ANY)] * 2,
-        scratch_shapes=[dma((8,))] * 8 + [dma((2,))],
+        scratch_shapes=[dma((4, CORNER_PARTS))] * 4 + [dma((2,))],
         compiler_params=pltpu.CompilerParams(collective_id=2, has_side_effects=True),
         cost_estimate=pl.CostEstimate(flops=0, bytes_accessed=60_000_000, transcendentals=0),
     )(last_rows)
@@ -381,43 +373,78 @@
     )(upper, lower, g, inverses)
 
 
-def column_kernel(row_count, chosen, out, send, recv, local_sem):
+def column_kernel(row_count, col_count, rest_ref, last_ref, out, send, recv, local_sem):
     row = lax.axis_index("row")
     col = lax.axis_index("col")
-    matrices, blocks, size, _ = chosen.shape
-    part = size // 4
+    matrices, blocks, size, _ = out.shape
+    part = size // COLUMN_PARTS
+    group = col_count // row_count
+    last_block = rest_ref.shape[1]
     greet([(r, col) for r in other_rows_of(row, row_count)])
-    place, after = chain_of(row, lax.rem(col, row_count), 0, row_count)
-
-    @pl.when(place == 0)
-    def _():
-        pltpu.make_async_copy(chosen, out, local_sem).start()
-
-    chunks = []
-    for b in range(blocks):
-        for p in range(4):
-            for m in range(matrices):
-                rows = pl.ds(p * part, part)
-                chunks.append((chosen.at[m, b, rows, :], out.at[m, b, rows, :]))
-    run_chains([(place, after, chunks, send, recv)], row, col, row_count, lambda which, n: None)
-
-    @pl.when(place == 0)
-    def _():
-        pltpu.make_async_copy(chosen, out, local_sem).wait()
-
-
-def share_columns(chosen, row_count):
-    count = chosen.shape[0] * chosen.shape[1] * 4
+    source = lax.rem(col, row_count)
+
+    def from_block(b, use):
+        block = col // row_count + b * group
+        if (b + 1) * group > last_block:
+
+            @pl.when(block == last_block)
+            def _():
+                use(last_ref)
+
+            @pl.when(block < last_block)
+            def _():
+                use(rest_ref.at[:, jnp.minimum(block, last_block - 1)])
+
+        else:
+            use(rest_ref.at[:, block])
+
+    pieces = [(b, p) for b in range(blocks) for p in range(COLUMN_PARTS)]
+    chains = []
+    for way in range(2):
+        place, after = chain_of(row, source, way, row_count)
+
+        def start(n, to, way=way):
+            b, p = pieces[n]
+            rows = pl.ds(p * part, part)
+            from_block(
+                b,
+                lambda src: remote(
+                    src.at[way, rows, :], out.at[way, b, rows, :],
+                    send.at[way, n], recv.at[way, n], to, col,
+                ).start(),
+            )
+
+        landings = [out.at[way, b, pl.ds(p * part, part), :] for b, p in pieces]
+        chains.append((place, after, start, landings, send.at[way], recv.at[way]))
+
+    def own(b, act):
+        from_block(b, lambda src: act(pltpu.make_async_copy(src, out.at[:, b], local_sem.at[b])))
+
+    @pl.when(row == source)
+    def _():
+        for b in range(blocks):
+            own(b, lambda copy: copy.start())
+
+    run_chains(chains, row, col, row_count, lambda which, n: None)
+
+    @pl.when(row == source)
+    def _():
+        for b in range(blocks):
+            own(b, lambda copy: copy.wait())
+
+
+def share_columns(rest, last, col_blocks, row_count, col_count):
+    matrices, _, size, width = rest.shape
     dma = pltpu.SemaphoreType.DMA
     return pl.pallas_call(
-        functools.partial(column_kernel, row_count),
-        out_shape=jax.ShapeDtypeStruct(chosen.shape, chosen.dtype),
-        in_specs=[pl.BlockSpec(memory_space=pl.ANY)],
+        functools.partial(column_kernel, row_count, col_count),
+        out_shape=jax.ShapeDtypeStruct((matrices, col_blocks, size, width), rest.dtype),
+        in_specs=[pl.BlockSpec(memory_space=pl.ANY)] * 2,
         out_specs=pl.BlockSpec(memory_space=pl.ANY),
-        scratch_shapes=[dma((count,)), dma((count,)), dma],
+        scratch_shapes=[dma((2, col_blocks * COLUMN_PARTS))] * 2 + [dma((col_blocks,))],
         compiler_params=pltpu.CompilerParams(collective_id=1, has_side_effects=True),
         cost_estimate=pl.CostEstimate(flops=0, bytes_accessed=60_000_000, transcendentals=0),
-    )(chosen)
+    )(rest, last)
 
 
 def update_kernel(
@@ -505,14 +532,7 @@
     rest = lax.all_gather(rest_here, "col", axis=2, tiled=True)
     upper, lower = share_corner(last, row_count)
     x = solve(upper, lower, g, inverses)
-    chosen = []
-    for b in range(col_blocks):
-        place = col_index // row_count + b * (col_count // row_count)
-        from_rest = lax.dynamic_index_in_dim(
-            rest, jnp.minimum(place, blocks_here - 2), 1, False
-        )
-        chosen.append(jnp.where(place == blocks_here - 1, last, from_rest))
-    cols = share_columns(jnp.stack(chosen, 1), row_count)
+    cols = share_columns(rest, last, col_blocks, row_count, col_count)
     new_rhs = update(rest, last, cols, x, rhs)
     rows_part = size // row_count
     cols_part = size // col_count

time: 420 us -> 407 us (0.969)
  the two profiles are of different devices: /device:TPU:19 before, /device:TPU:18 now
where the time goes in v3:
time: 407 us
  Pallas kernels  384 us (94%)
  between operations  14.1 us (3%)
  local copies, waits for them, and re-layouts  9 us (2%)
    pallas_call x1, Pallas kernels, share_columns(): pl.pallas_call(functools.partial(column_kernel, row_count, col_count), ou...  203 us
    pallas_call x1, Pallas kernels, share_corner(): pl.pallas_call(functools.partial(corner_kernel, row_count), out_shape=(ja...  75.3 us
    pallas_call x1, Pallas kernels, share_g(): pl.pallas_call(functools.partial(g_kernel, row_count, col_count), out_sha...  59 us
    pallas_call x1, Pallas kernels, solve(): pl.pallas_call(solve_kernel, out_shape=jax.ShapeDtypeStruct((2, size, siz...  25 us
    pallas_call x1, Pallas kernels, update(): pl.pallas_call(functools.partial(update_kernel, rest_steps), grid=(steps,...  21.5 us
  transfers between devices with their start and end apart: 2, of which 0 were waited for; matrix products, arithmetic and copies ran while one was open for 1% of the time, Pallas kernels for 39%

profile of v3, /device:TPU:18, one launch (start us, length us, event | category | flops | bytes accessed | tf_op | source)
XLA Modules:
  0.0 406.9 jit_solution(7762681967457201533)
XLA Ops:
  7.2 0.0 all-gather.6.cloned.1.call-start
  7.2 1.7 slice_bitcast_fusion.1
  8.9 0.0 all-gather.6.cloned.1.call-update
  9.0 0.0 all-gather.4.cloned.1.call-start
  9.0 1.9 slice.11
  11.0 0.0 copy-start.3
  11.0 1.0 copy.13
  12.0 59.0 %shard_map.50.g = f32[2,512,512]{2,1,0:T(8,128)} custom-call(f32[512,512]{1,0:T(8,128)} %bitcast.18), custom_call_target="tpu_custom_call" | custom-call | bytes 60000000 | tf_op jit(solution)/shard_map/pallas_call | solution.py:136
  71.0 0.0 copy-done.3
  71.0 0.9 slice_bitcast_fusion
  71.9 0.0 all-gather.6.cloned.1.call-done
  71.9 0.0 all-gather.4.cloned.1.call-update
  72.0 75.3 %shard_map.52 = (bf16[2,512,1024]{2,1,0:T(8,128)(2,1)}, bf16[2,512,512]{2,1,0:T(8,128)(2,1)}) custom-call(bf16[2,512,1024]{2,1,0:T(8,128)(2,1)} %bitcast.12), custom_call_target="tpu_custom_call" | custom-call | bytes 60000000 | tf_op jit(solution)/shard_map/pallas_call | solution.py:262
  147.3 0.0 copy-start.2
  147.3 1.2 copy-done.2
  148.5 25.0 %shard_map.53.x_ref = f32[2,512,512]{2,1,0:T(8,128)S(1)} custom-call(bf16[2,512,1024]{2,1,0:T(8,128)(2,1)} %get-tuple-element.9.upper, bf16[2,512,512]{2,1,0:T(8,128)(2,1)S(1)} %copy-done.2, f32[2,512,512]{2,1,0:T(8,128)} %shard_map.50.g, f32[3,512,512]{2,1,0:T(8,128)} %inverses.1), custom_call_target="tpu_custom_call" | custom-call | flops 13421772800 | bytes 100000000 | tf_op jit(solution)/shard_map/pallas_call | solution.py:360
  173.6 0.0 copy-start.1
  173.6 1.3 copy-done.1
  174.9 0.1 constant_dynamic-slice_fusion
  175.0 0.7 copy.9
  175.7 0.0 copy-start
  175.7 0.0 all-gather.4.cloned.1.call-done.rest_ref
  175.7 202.8 %shard_map.51.cols_ref = bf16[2,2,512,1024]{3,2,1,0:T(8,128)(2,1)} custom-call(bf16[2,3,512,1024]{3,2,1,0:T(8,128)(2,1)} %all-gather.4.cloned.1.call-done.rest_ref, bf16[2,512,1024]{2,1,0:T(8,128)(2,1)} %bitcast.13), custom_call_target="tpu_custom_call" | custom-call | bytes 60000000 | tf_op jit(solution)/shard_map/pallas_call | solution.py:439
  378.5 0.0 copy-done
  378.6 21.5 %shard_map.54 = f32[16384,128]{1,0:T(8,128)} custom-call(bf16[2,1536,1024]{2,1,0:T(8,128)(2,1)} %bitcast.15, bf16[2,512,1024]{2,1,0:T(8,128)(2,1)S(1)} %bitcast.14, bf16[2,2,512,1024]{3,2,1,0:T(8,128)(2,1)} %shard_map.51.cols_ref, f32[2,512,512]{2,1,0:T(8,128)} %copy-done.1, f32[16384,128]{1,0:T(8,128)} %bitcast.16), custom_call_target="tpu_custom_call" | custom-call | tf_op jit(solution)/shard_map/pallas_call | solution.py:498
Async XLA Ops:
  7.2 64.8 %all-gather.6.cloned.1.call-start = ((), (), s32[]{:S(2)}) async-start(), calls=%async_computation.1 | async-start | bytes 2359296 | tf_op jit(solution)/shard_map/all_gather | solution.py:528
  9.0 166.8 %all-gather.4.cloned.1.call-start = ((), (), s32[]{:S(2)}) async-start(), calls=%async_computation | async-start | bytes 7077888 | tf_op jit(solution)/shard_map/all_gather | solution.py:532
  11.0 60.0 %copy-start.3 = (bf16[2,4,1,64,1024]{4,3,2,1,0:T(8,128)(2,1)S(1)}, bf16[2,4,1,64,1024]{4,3,2,1,0:T(8,128)(2,1)}, u32[]{:S(2)}) copy-start(bf16[2,4,1,64,1024]{4,3,2,1,0:T(8,128)(2,1)} %param.4) | copy-start | bytes 3145732
  147.3 1.2 copy-start.2
  173.6 1.3 copy-start.1
  175.7 202.8 %copy-start = (bf16[2,1,1,512,1024]{4,3,0,2,1:T(8,128)(2,1)S(1)}, bf16[2,1,1,512,1024]{4,3,0,2,1:T(8,128)(2,1)}, u32[]{:S(2)}) copy-start(bf16[2,1,1,512,1024]{4,3,0,2,1:T(8,128)(2,1)} %all-gather.6.cloned.1.call-done) | copy-start | bytes 6291460
Sparse Core Ops, SparseCore 0:
  9.6 43.4 all-gather.5
  72.1 62.5 all-gather.3

commit v4 on v3

--- a/solution.py
+++ b/solution.py
@@ -137,12 +137,14 @@
         functools.partial(g_kernel, row_count, col_count),
         out_shape=jax.ShapeDtypeStruct((2, size, size), jnp.float32),
         in_specs=[pl.BlockSpec(memory_space=pl.ANY)],
-        out_specs=pl.BlockSpec(memory_space=pl.ANY),
+        out_specs=pl.BlockSpec(memory_space=pltpu.VMEM),
         scratch_shapes=[
             dma((2, 2 * peers + 1)), dma((col_count // 2,)), dma((peers,)), dma((row_count,)),
             dma((2,)), dma, dma((row_count,)), dma((row_count,)), dma((2,)),
         ],
-        compiler_params=pltpu.CompilerParams(collective_id=0, has_side_effects=True),
+        compiler_params=pltpu.CompilerParams(
+            collective_id=0, has_side_effects=True, vmem_limit_bytes=VMEM_LIMIT
+        ),
         cost_estimate=pl.CostEstimate(flops=0, bytes_accessed=60_000_000, transcendentals=0),
     )(rhs_last)
 
@@ -266,9 +268,11 @@
             jax.ShapeDtypeStruct((2, size, size), jnp.bfloat16),
         ),
         in_specs=[pl.BlockSpec(memory_space=pl.ANY)],
-        out_specs=[pl.BlockSpec(memory_space=pl.ANY)] * 2,
+        out_specs=[pl.BlockSpec(memory_space=pltpu.VMEM)] * 2,
         scratch_shapes=[dma((4, CORNER_PARTS))] * 4 + [dma((2,))],
-        compiler_params=pltpu.CompilerParams(collective_id=2, has_side_effects=True),
+        compiler_params=pltpu.CompilerParams(
+            collective_id=2, has_side_effects=True, vmem_limit_bytes=VMEM_LIMIT
+        ),
         cost_estimate=pl.CostEstimate(flops=0, bytes_accessed=60_000_000, transcendentals=0),
     )(last_rows)
 
@@ -440,9 +444,11 @@
         functools.partial(column_kernel, row_count, col_count),
         out_shape=jax.ShapeDtypeStruct((matrices, col_blocks, size, width), rest.dtype),
         in_specs=[pl.BlockSpec(memory_space=pl.ANY)] * 2,
-        out_specs=pl.BlockSpec(memory_space=pl.ANY),
+        out_specs=pl.BlockSpec(memory_space=pltpu.VMEM),
         scratch_shapes=[dma((2, col_blocks * COLUMN_PARTS))] * 2 + [dma((col_blocks,))],
-        compiler_params=pltpu.CompilerParams(collective_id=1, has_side_effects=True),
+        compiler_params=pltpu.CompilerParams(
+            collective_id=1, has_side_effects=True, vmem_limit_bytes=VMEM_LIMIT
+        ),
         cost_estimate=pl.CostEstimate(flops=0, bytes_accessed=60_000_000, transcendentals=0),
     )(rest, last)
 

time: 407 us -> 398 us (0.978)
  Pallas kernels: 384 us -> 374 us
    pallas_call x1, Pallas kernels: 203 us -> 195 us  [share_columns(): pl.pallas_call(functools.partial(column_kernel, row_count, col_count), ou...]
where the time goes in v4:
time: 398 us
  Pallas kernels  374 us (94%)
  between operations  14.1 us (4%)
  local copies, waits for them, and re-layouts  9.54 us (2%)
    pallas_call x1, Pallas kernels, share_columns(): pl.pallas_call(functools.partial(column_kernel, row_count, col_count), ou...  195 us
    pallas_call x1, Pallas kernels, share_corner(): pl.pallas_call(functools.partial(corner_kernel, row_count), out_shape=(ja...  72.1 us
    pallas_call x1, Pallas kernels, share_g(): pl.pallas_call(functools.partial(g_kernel, row_count, col_count), out_sha...  59.8 us
    pallas_call x1, Pallas kernels, solve(): pl.pallas_call(solve_kernel, out_shape=jax.ShapeDtypeStruct((2, size, siz...  25.2 us
    pallas_call x1, Pallas kernels, update(): pl.pallas_call(functools.partial(update_kernel, rest_steps), grid=(steps,...  21.5 us
  transfers between devices with their start and end apart: 2, of which 0 were waited for; matrix products, arithmetic and copies ran while one was open for 1% of the time, Pallas kernels for 39%

profile of v4, /device:TPU:18, one launch (start us, length us, event | category | flops | bytes accessed | tf_op | source)
XLA Modules:
  0.0 397.7 jit_solution(18121458420539927357)
XLA Ops:
  7.2 0.0 all-gather.6.cloned.1.call-start
  7.2 1.7 slice_bitcast_fusion.1
  8.9 0.0 all-gather.6.cloned.1.call-update
  8.9 0.0 all-gather.4.cloned.1.call-start
  9.0 1.9 slice.11
  10.9 0.0 copy-start.4
  10.9 0.1 copy.13
  11.0 59.8 %shard_map.50.g = f32[2,512,512]{2,1,0:T(8,128)S(1)} custom-call(f32[512,512]{1,0:T(8,128)S(1)} %bitcast.15), custom_call_target="tpu_custom_call" | custom-call | bytes 60000000 | tf_op jit(solution)/shard_map/pallas_call | solution.py:136
  70.9 0.0 copy-start.2
  70.9 1.4 copy-done.2
  72.2 0.0 copy-done.4
  72.2 1.0 slice_bitcast_fusion
  73.3 0.0 all-gather.6.cloned.1.call-done
  73.3 0.0 all-gather.4.cloned.1.call-update
  73.3 72.1 %shard_map.52 = (bf16[2,512,1024]{2,1,0:T(8,128)(2,1)S(1)}, bf16[2,512,512]{2,1,0:T(8,128)(2,1)S(1)}) custom-call(bf16[2,512,1024]{2,1,0:T(8,128)(2,1)} %bitcast.12), custom_call_target="tpu_custom_call" | custom-call | bytes 60000000 | tf_op jit(solution)/shard_map/pallas_call | solution.py:264
  145.4 0.0 copy-start.3
  145.4 1.3 copy-done.3
  146.7 0.0 copy-start
  146.7 25.2 %shard_map.53.x_ref = f32[2,512,512]{2,1,0:T(8,128)S(1)} custom-call(bf16[2,512,1024]{2,1,0:T(8,128)(2,1)} %copy-done.3, bf16[2,512,512]{2,1,0:T(8,128)(2,1)S(1)} %get-tuple-element.10.lower, f32[2,512,512]{2,1,0:T(8,128)} %copy-done.2, f32[3,512,512]{2,1,0:T(8,128)} %inverses.1), custom_call_target="tpu_custom_call" | custom-call | flops 13421772800 | bytes 100000000 | tf_op jit(solution)/shard_map/pallas_call | solution.py:364
  171.9 0.0 copy-start.1
  171.9 1.3 copy-done.1
  173.2 0.1 constant_dynamic-slice_fusion
  173.3 0.7 copy.9
  174.0 0.0 all-gather.4.cloned.1.call-done.rest_ref
  174.0 0.0 copy-done
  174.0 195.3 %shard_map.51.cols_ref = bf16[2,2,512,1024]{3,2,1,0:T(8,128)(2,1)} custom-call(bf16[2,3,512,1024]{3,2,1,0:T(8,128)(2,1)} %all-gather.4.cloned.1.call-done.rest_ref, bf16[2,512,1024]{2,1,0:T(8,128)(2,1)S(1)} %bitcast.13), custom_call_target="tpu_custom_call" | custom-call | bytes 60000000 | tf_op jit(solution)/shard_map/pallas_call | solution.py:443
  369.4 21.5 %shard_map.54 = f32[16384,128]{1,0:T(8,128)} custom-call(bf16[2,1536,1024]{2,1,0:T(8,128)(2,1)} %bitcast.16, bf16[2,512,1024]{2,1,0:T(8,128)(2,1)S(1)} %bitcast.14, bf16[2,2,512,1024]{3,2,1,0:T(8,128)(2,1)} %shard_map.51.cols_ref, f32[2,512,512]{2,1,0:T(8,128)} %copy-done.1, f32[16384,128]{1,0:T(8,128)} %bitcast.17), custom_call_target="tpu_custom_call" | custom-call | tf_op jit(solution)/shard_map/pallas_call | solution.py:504
Async XLA Ops:
  7.2 66.1 %all-gather.6.cloned.1.call-start = ((), (), s32[]{:S(2)}) async-start(), calls=%async_computation.1 | async-start | bytes 2359296 | tf_op jit(solution)/shard_map/all_gather | solution.py:534
  8.9 165.1 %all-gather.4.cloned.1.call-start = ((), (), s32[]{:S(2)}) async-start(), calls=%async_computation | async-start | bytes 7077888 | tf_op jit(solution)/shard_map/all_gather | solution.py:538
  10.9 61.3 %copy-start.4 = (bf16[2,4,1,64,1024]{4,3,2,1,0:T(8,128)(2,1)S(1)}, bf16[2,4,1,64,1024]{4,3,2,1,0:T(8,128)(2,1)}, u32[]{:S(2)}) copy-start(bf16[2,4,1,64,1024]{4,3,2,1,0:T(8,128)(2,1)} %param.4) | copy-start | bytes 3145732
  70.9 1.4 copy-start.2
  145.4 1.3 copy-start.3
  146.7 27.3 %copy-start = (bf16[2,1,1,512,1024]{4,3,0,2,1:T(8,128)(2,1)S(1)}, bf16[2,1,1,512,1024]{4,3,0,2,1:T(8,128)(2,1)}, u32[]{:S(2)}) copy-start(bf16[2,1,1,512,1024]{4,3,0,2,1:T(8,128)(2,1)} %all-gather.6.cloned.1.call-done) | copy-start | bytes 6291460
  171.9 1.3 copy-start.1
Sparse Core Ops, SparseCore 0:
  10.2 45.6 all-gather.5
  73.4 62.5 all-gather.3

commit v5 on v4

--- a/solution.py
+++ b/solution.py
@@ -170,19 +170,19 @@
             def _():
                 start(n, after)
 
-    for n in range(len(chains[0][3])):
+    count = len(chains[0][3])
+    for step in range(1, count + row_count - 1):
         for which, (place, after, start, landings, send, recv) in enumerate(chains):
-            dst = landings[n]
-
-            @pl.when(place > 0)
-            def _():
-                remote(dst, dst, send.at[n], recv.at[n], after, col).wait_recv()
-
-                @pl.when(place < row_count - 1)
+            for at in range(max(1, step - count + 1), min(step, row_count - 1) + 1):
+                n = step - at
+                dst = landings[n]
+
+                @pl.when(place == at)
                 def _():
-                    remote(dst, dst, send.at[n], recv.at[n], after, col).start()
-
-                on_arrival(which, n)
+                    remote(dst, dst, send.at[n], recv.at[n], after, col).wait_recv()
+                    if at < row_count - 1:
+                        remote(dst, dst, send.at[n], recv.at[n], after, col).start()
+                    on_arrival(which, n)
 
     for place, after, start, landings, send, recv in chains:
 

time: 398 us -> 234 us (0.59)
  Pallas kernels: 374 us -> 206 us
    pallas_call x1, Pallas kernels: 195 us -> 67.7 us  [share_columns(): pl.pallas_call(functools.partial(column_kernel, row_count, col_count), ou...]
    pallas_call x1, Pallas kernels: 72.1 us -> 32.2 us  [share_corner(): pl.pallas_call(functools.partial(corner_kernel, row_count), out_shape=(ja...]
  transfers between devices with their start and end apart: 2 -> 2, of which waited for: 0 -> 1; matrix products, arithmetic and copies ran while one was open for 1% -> 2% of each run, Pallas kernels for 39% -> 51%
where the time goes in v5:
time: 234 us; the launch traced here: 232 us
  Pallas kernels  206 us (88%)
  between operations  14.1 us (6%)
  local copies, waits for them, and re-layouts  9.54 us (4%)
    pallas_call x1, Pallas kernels, share_columns(): pl.pallas_call(functools.partial(column_kernel, row_count, col_count), ou...  67.7 us
    pallas_call x1, Pallas kernels, share_g(): pl.pallas_call(functools.partial(g_kernel, row_count, col_count), out_sha...  59.8 us
    pallas_call x1, Pallas kernels, share_corner(): pl.pallas_call(functools.partial(corner_kernel, row_count), out_shape=(ja...  32.2 us
    pallas_call x1, Pallas kernels, solve(): pl.pallas_call(solve_kernel, out_shape=jax.ShapeDtypeStruct((2, size, siz...  25.2 us
    pallas_call x1, Pallas kernels, update(): pl.pallas_call(functools.partial(update_kernel, rest_steps), grid=(steps,...  21.5 us
    unnamed x13, local copies, waits for them, and re-layouts  6.47 us
  transfers between devices with their start and end apart: 2, of which 1 were waited for; matrix products, arithmetic and copies ran while one was open for 2% of the time, Pallas kernels for 51%

profile of v5, /device:TPU:18, one launch (start us, length us, event | category | flops | bytes accessed | tf_op | source)
XLA Modules:
  0.0 232.1 jit_solution(17553669457488097108)
XLA Ops:
  7.2 0.0 all-gather.6.cloned.1.call-start
  7.2 1.7 slice_bitcast_fusion.1
  8.9 0.0 all-gather.6.cloned.1.call-update
  8.9 0.0 all-gather.4.cloned.1.call-start
  9.0 1.9 slice.11
  10.9 0.0 copy-start.4
  10.9 0.1 copy.13
  11.0 59.8 %shard_map.50.g = f32[2,512,512]{2,1,0:T(8,128)S(1)} custom-call(f32[512,512]{1,0:T(8,128)S(1)} %bitcast.15), custom_call_target="tpu_custom_call" | custom-call | bytes 60000000 | tf_op jit(solution)/shard_map/pallas_call | solution.py:136
  70.9 0.0 copy-start.2
  70.9 1.4 copy-done.2
  72.2 0.0 copy-done.4
  72.2 1.0 slice_bitcast_fusion
  73.3 0.0 all-gather.6.cloned.1.call-done
  73.3 0.0 all-gather.4.cloned.1.call-update
  73.3 32.2 %shard_map.52 = (bf16[2,512,1024]{2,1,0:T(8,128)(2,1)S(1)}, bf16[2,512,512]{2,1,0:T(8,128)(2,1)S(1)}) custom-call(bf16[2,512,1024]{2,1,0:T(8,128)(2,1)} %bitcast.12), custom_call_target="tpu_custom_call" | custom-call | bytes 60000000 | tf_op jit(solution)/shard_map/pallas_call | solution.py:264
  105.5 0.0 copy-start.3
  105.5 1.3 copy-done.3
  106.8 0.0 copy-start
  106.8 25.2 %shard_map.53.x_ref = f32[2,512,512]{2,1,0:T(8,128)S(1)} custom-call(bf16[2,512,1024]{2,1,0:T(8,128)(2,1)} %copy-done.3, bf16[2,512,512]{2,1,0:T(8,128)(2,1)S(1)} %get-tuple-element.10.lower, f32[2,512,512]{2,1,0:T(8,128)} %copy-done.2, f32[3,512,512]{2,1,0:T(8,128)} %inverses.1), custom_call_target="tpu_custom_call" | custom-call | flops 13421772800 | bytes 100000000 | tf_op jit(solution)/shard_map/pallas_call | solution.py:364
  132.0 0.0 copy-start.1
  132.0 1.3 copy-done.1
  133.3 0.1 constant_dynamic-slice_fusion
  133.4 0.7 copy.9
  134.1 1.8 all-gather.4.cloned.1.call-done.rest_ref
  136.0 0.0 copy-done
  136.0 67.7 %shard_map.51.cols_ref = bf16[2,2,512,1024]{3,2,1,0:T(8,128)(2,1)} custom-call(bf16[2,3,512,1024]{3,2,1,0:T(8,128)(2,1)} %all-gather.4.cloned.1.call-done.rest_ref, bf16[2,512,1024]{2,1,0:T(8,128)(2,1)S(1)} %bitcast.13), custom_call_target="tpu_custom_call" | custom-call | bytes 60000000 | tf_op jit(solution)/shard_map/pallas_call | solution.py:443
  203.7 21.5 %shard_map.54 = f32[16384,128]{1,0:T(8,128)} custom-call(bf16[2,1536,1024]{2,1,0:T(8,128)(2,1)} %bitcast.16, bf16[2,512,1024]{2,1,0:T(8,128)(2,1)S(1)} %bitcast.14, bf16[2,2,512,1024]{3,2,1,0:T(8,128)(2,1)} %shard_map.51.cols_ref, f32[2,512,512]{2,1,0:T(8,128)} %copy-done.1, f32[16384,128]{1,0:T(8,128)} %bitcast.17), custom_call_target="tpu_custom_call" | custom-call | tf_op jit(solution)/shard_map/pallas_call | solution.py:504
Async XLA Ops:
  7.2 66.1 %all-gather.6.cloned.1.call-start = ((), (), s32[]{:S(2)}) async-start(), calls=%async_computation.1 | async-start | bytes 2359296 | tf_op jit(solution)/shard_map/all_gather | solution.py:534
  8.9 127.1 %all-gather.4.cloned.1.call-start = ((), (), s32[]{:S(2)}) async-start(), calls=%async_computation | async-start | bytes 7077888 | tf_op jit(solution)/shard_map/all_gather | solution.py:538
  10.9 61.3 %copy-start.4 = (bf16[2,4,1,64,1024]{4,3,2,1,0:T(8,128)(2,1)S(1)}, bf16[2,4,1,64,1024]{4,3,2,1,0:T(8,128)(2,1)}, u32[]{:S(2)}) copy-start(bf16[2,4,1,64,1024]{4,3,2,1,0:T(8,128)(2,1)} %param.4) | copy-start | bytes 3145732
  70.9 1.4 copy-start.2
  105.5 1.3 copy-start.3
  106.8 29.2 %copy-start = (bf16[2,1,1,512,1024]{4,3,0,2,1:T(8,128)(2,1)S(1)}, bf16[2,1,1,512,1024]{4,3,0,2,1:T(8,128)(2,1)}, u32[]{:S(2)}) copy-start(bf16[2,1,1,512,1024]{4,3,0,2,1:T(8,128)(2,1)} %all-gather.6.cloned.1.call-done) | copy-start | bytes 6291460
  132.0 1.3 copy-start.1
Sparse Core Ops, SparseCore 0:
  10.2 45.6 all-gather.5
  73.4 62.5 all-gather.3
